TPU v7x, 512 devices: a whole 4x8x8 slice. The times are simulated.
512 devices in a mesh: vertex: 64 (over x, z, core), feat: 8 (over y).
Axes of the slice: x: 4, y: 8, z: 8, core: 2. Of those that a mesh axis runs over, the one named last changes fastest.
Arguments:
- node_feats: bfloat16 [65536, 128], P('vertex', 'feat'), may hold values from -6 to 6
- adj_tiles: bfloat16 [512, 6, 128, 128], P('vertex'), may hold values from 0 to 1
- tile_cols: int32 [512, 6], P('vertex'), may hold values from 0 to 511, as said below
- degrees: int32 [65536], P('vertex'), may hold values from 8 to 64
- w_self: bfloat16 [128, 256], P('feat'), may hold values from -0.375 to 0.375
- w_neigh: bfloat16 [128, 256], P('feat'), may hold values from -0.375 to 0.375
- hidden_bias: float32 [256], replicated, may hold values from -3 to 3
- cotangent: bfloat16 [65536, 256], P(('vertex', 'feat')), may hold values from -6 to 6
Outputs:
- hidden: bfloat16 [65536, 256], P(('vertex', 'feat'))
- grad_self: float32 [128, 256], P('feat')
- grad_neigh: float32 [128, 256], P('feat')
- grad_bias: float32 [256], replicated
Inputs may be any that keep to these rules, and one draw needn't show every extreme that they name: `tile_cols`: row block r lies on vertex index r // 8; each of its tiles' column blocks lies on the same vertex index or on one of the two next to it, cyclically (index 0 next to the last).
All inputs are finite; a program needn't handle non-finite values.
Results may differ from a plain program's by a relative error of at most 0.019.
Values may be sent and summed in bfloat16 or wider, within the bound.
No kernel may reach another device: no remote copies, remote signals or barrier semaphores. Data moves between devices by JAX's collectives and lax.ppermute only.
A program may use at most 64 MiB of HBM per device.

v0:
```python
import jax
import jax.numpy as jnp
from jax import lax
from jax.sharding import PartitionSpec as P


def extended_2(block, sides, width):
    for axis, dim in sides:
        count = lax.axis_size(axis)
        forward = [(i, i + 1) for i in range(count - 1)]
        forward.append((count - 1, 0))
        backward = [(target, source) for source, target in forward]
        low = lax.ppermute(
            lax.slice_in_dim(block, block.shape[dim] - width, None, axis=dim), axis, forward
        )
        high = lax.ppermute(lax.slice_in_dim(block, 0, width, axis=dim), axis, backward)
        block = jnp.concatenate([low, block, high], axis=dim)
    return block


def shards(node_feats, adj_tiles, tile_cols, degrees, w_self, w_neigh, hidden_bias, cotangent):
    node_count = node_feats.shape[0]
    feat_local = node_feats.shape[1]
    blk_here = adj_tiles.shape[0]
    tile_size = adj_tiles.shape[2]
    vertex_count = lax.axis_size("vertex")
    extended = extended_2(node_feats, (("vertex", 0),), node_count)
    blocks = extended.reshape(3 * blk_here, tile_size, feat_local)
    vertex_idx = lax.axis_index("vertex")
    local_cols = (tile_cols - vertex_idx * blk_here + blk_here) % (blk_here * vertex_count)
    picked = blocks[local_cols]
    summed = jnp.einsum("bkij,bkjf->bif", adj_tiles, picked, preferred_element_type=jnp.float32)
    summed = summed.reshape(node_count, feat_local)
    averaged = (summed / degrees.astype(jnp.float32)[:, None]).astype(jnp.bfloat16)
    feat_rows = node_feats
    mean_rows = averaged
    preact = (
        lax.psum_scatter(
            jnp.dot(feat_rows, w_self, preferred_element_type=jnp.float32)
            + jnp.dot(mean_rows, w_neigh, preferred_element_type=jnp.float32),
            "feat",
            scatter_dimension=0,
            tiled=True,
        )
        + hidden_bias
    )
    hidden = jnp.maximum(preact, 0.0).astype(jnp.bfloat16)
    grad_pre = jnp.where(preact > 0, cotangent, jnp.zeros_like(cotangent))
    piece = lax.all_gather(grad_pre, "feat", axis=0, tiled=True)
    feat_rows = node_feats
    mean_rows = averaged
    grad_self, grad_neigh, grad_bias = lax.psum(
        (
            jnp.einsum("rf,rh->fh", feat_rows, piece, preferred_element_type=jnp.float32),
            jnp.einsum("rf,rh->fh", mean_rows, piece, preferred_element_type=jnp.float32),
            jnp.sum(piece.astype(jnp.float32), axis=0),
        ),
        "vertex",
    )
    return (hidden, grad_self, grad_neigh, grad_bias)


def solution(mesh):
    return jax.shard_map(
        shards,
        mesh=mesh,
        in_specs=(
            P("vertex", "feat"),
            P("vertex", None, None, None),
            P("vertex", None),
            P("vertex"),
            P("feat", None),
            P("feat", None),
            P(),
            P(("vertex", "feat"), None),
        ),
        out_specs=(P(("vertex", "feat"), None), P("feat", None), P("feat", None), P()),
        check_vma=False,
    )
```

profile of v0, /device:TPU:1, one launch (start us, length us, event | category | flops | bytes accessed | tf_op | source)
XLA Modules:
  0.0 345.0 jit_solution(17646538898353907636)
XLA Ops:
  7.2 0.0 copy-start
  7.2 0.0 reduce-scatter.2.cloned.1.call-start
  7.2 8.9 %collective-permute-start.1 = (bf16[1024,16]{0,1:T(8,128)(2,1)}, bf16[1024,16]{0,1:T(8,128)(2,1)S(1)}, u32[]{:S(2)}, u32[]{:S(2)}) collective-permute-start(bf16[1024,16]{0,1:T(8,128)(2,1)} %param.8), channel_id=1, source_target_pairs={{8,0},{16,8},{24,16},{32,24},{40,32},{48,40},{56,48},{64,56},{72,6... | collective-permute-start | bytes 98312 | tf_op jit(solution)/shard_map/ppermute | solution.py:16
  16.2 1.9 collective-permute-start
  18.1 0.7 compare_select_fusion.1
  18.8 0.1 reshape.20
  18.9 1.1 fusion.5
  20.0 0.7 convert_element_type.12
  20.7 0.0 collective-permute-done.1
  20.7 3.6 %collective-permute-done = bf16[1024,16]{0,1:T(8,128)(2,1)S(1)} collective-permute-done((bf16[1024,16]{0,1:T(8,128)(2,1)}, bf16[1024,16]{0,1:T(8,128)(2,1)S(1)}, u32[]{:S(2)}, u32[]{:S(2)}) %collective-permute-start) | collective-permute-done | bytes 32800 | tf_op jit(solution)/shard_map/ppermute | solution.py:13
  24.3 0.8 copy_bitcast_fusion
  25.0 0.6 gather_fusion
  25.7 0.0 copy-start.4
  25.7 0.0 copy-done
  25.7 0.5 convolution_bitcast_fusion
  26.2 0.2 copy-done.4
  26.4 0.0 copy-start.3
  26.4 0.0 copy-start.5
  26.4 1.3 convolution_add_fusion
  27.7 0.0 copy-start.2
  27.7 0.0 reduce-scatter.2.cloned.1.call-update
  27.7 36.1 %reduce-scatter.2.cloned.1.call-done = f32[128,256]{1,0:T(8,128)} async-done(((f32[1024,256]{1,0:T(8,128)}), f32[128,256]{1,0:T(8,128)}) %reduce-scatter.2.cloned.1.call-update) | async-done | bytes 131088 | tf_op jit(solution)/shard_map/reduce_scatter | solution.py:38
  63.8 0.0 copy-done.3
  63.8 0.0 copy-done.5
  63.8 0.0 copy-start.1
  63.8 1.0 compare_select_fusion
  64.8 19.8 %all_gather.3 = bf16[1024,256]{1,0:T(8,128)(2,1)S(1)} all-gather(bf16[128,256]{1,0:T(8,128)(2,1)S(1)} %compare_select_fusion), channel_id=1, replica_groups=mesh['vertex'=64,'feat'=8] {'feat'}, dimensions={0}, use_global_device_ids=true | all-gather | bytes 589824 | tf_op jit(solution)/shard_map/all_gather | solution.py:49
  84.6 0.2 fusion.2
  84.8 0.2 convert_reduce_fusion
  85.0 0.0 copy-done.2
  85.0 0.2 convolution_bitcast_fusion.1
  85.1 252.4 %all-reduce = (f32[16,256]{1,0:T(8,128)}, f32[16,256]{1,0:T(8,128)}, f32[256]{0:T(256)}) all-reduce(f32[16,256]{1,0:T(8,128)S(1)} %convolution_bitcast_fusion.1, f32[16,256]{1,0:T(8,128)S(1)} %fusion.2, f32[256]{0:T(256)S(1)} %convert_reduce_fusion), channel_id=1, replica_groups=mesh['vertex'=64,'feat'=8] {'vertex'}, use_global_device_ids=true, to_apply=%region_1.2 | all-reduce | flops 8448 | bytes 67584 | tf_op jit(solution)/shard_map/psum | solution.py:52
  337.5 0.0 copy-done.1
  337.5 0.6 maximum_convert_fusion
  (1 shorter events, 0.0 us)
Async XLA Ops:
  7.2 18.5 %copy-start = (bf16[8,6,128,128]{3,2,1,0:T(8,128)(2,1)S(1)}, bf16[8,6,128,128]{3,2,1,0:T(8,128)(2,1)}, u32[]{:S(2)}) copy-start(bf16[8,6,128,128]{3,2,1,0:T(8,128)(2,1)} %param.9) | copy-start | bytes 4718596
  7.2 56.6 %reduce-scatter.2.cloned.1.call-start = ((), (), s32[]{:S(2)}) async-start(), calls=%async_computation.1 | async-start | bytes 1179648 | tf_op jit(solution)/shard_map/reduce_scatter | solution.py:38
  7.2 13.4 %collective-permute-start.1 = (bf16[1024,16]{0,1:T(8,128)(2,1)}, bf16[1024,16]{0,1:T(8,128)(2,1)S(1)}, u32[]{:S(2)}, u32[]{:S(2)}) collective-permute-start(bf16[1024,16]{0,1:T(8,128)(2,1)} %param.8), channel_id=1, source_target_pairs={{8,0},{16,8},{24,16},{32,24},{40,32},{48,40},{56,48},{64,56},{72,6... | collective-permute-start | bytes 98312 | tf_op jit(solution)/shard_map/ppermute | solution.py:16
  16.2 8.1 %collective-permute-start = (bf16[1024,16]{0,1:T(8,128)(2,1)}, bf16[1024,16]{0,1:T(8,128)(2,1)S(1)}, u32[]{:S(2)}, u32[]{:S(2)}) collective-permute-start(bf16[1024,16]{0,1:T(8,128)(2,1)} %param.8), channel_id=1, source_target_pairs={{0,8},{8,16},{16,24},{24,32},{32,40},{40,48},{48,56},{56,64},{64,7... | collective-permute-start | bytes 98312 | tf_op jit(solution)/shard_map/ppermute | solution.py:13
  25.7 0.7 copy-start.4
  26.4 37.4 %copy-start.3 = (bf16[128,256]{1,0:T(8,128)(2,1)S(1)}, bf16[128,256]{1,0:T(8,128)(2,1)}, u32[]{:S(2)}) copy-start(bf16[128,256]{1,0:T(8,128)(2,1)} %param.15) | copy-start | bytes 196612
  26.4 37.4 %copy-start.5 = (f32[256]{0:T(256)S(1)}, f32[256]{0:T(256)}, u32[]{:S(2)}) copy-start(f32[256]{0:T(256)} %param.14) | copy-start | bytes 3076
  27.7 57.3 %copy-start.2 = (bf16[1024,16]{0,1:T(8,128)(2,1)S(1)}, bf16[1024,16]{0,1:T(8,128)(2,1)}, u32[]{:S(2)}) copy-start(bf16[1024,16]{0,1:T(8,128)(2,1)} %param.8) | copy-start | bytes 98308
  63.8 273.7 %copy-start.1 = (f32[128,256]{1,0:T(8,128)S(1)}, f32[128,256]{1,0:T(8,128)}, u32[]{:S(2)}) copy-start(f32[128,256]{1,0:T(8,128)} %reduce-scatter.2.cloned.1.call-done) | copy-start | bytes 393220
Sparse Core Ops, SparseCore 0:
  27.8 35.9 reduce-scatter.1
where the time goes:
time: 349 us; the launch traced here: 345 us
  blocking collectives  272 us (78%)
  waiting for transfers between devices  39.7 us (11%)
  between operations  14.1 us (4%)
  starting transfers between devices  10.9 us (3%)
  other arithmetic  3.97 us (1%)
    psum x1, blocking collectives, shards(): lax.psum((jnp.einsum('rf,rh->fh', feat_rows, piece, preferred_element_typ...  252 us
    reduce_scatter x1, waiting for transfers between devices, shards(): lax.psum_scatter(jnp.dot(feat_rows, w_self, preferred_element_type=jnp.fl...  36.1 us
    all_gather x1, blocking collectives, shards(): piece = lax.all_gather(grad_pre, 'feat', axis=0, tiled=True)  19.8 us
    ppermute x1, starting transfers between devices, extended_2(): lax.ppermute(lax.slice_in_dim(block, 0, width, axis=dim), axis, backward)  8.92 us
  transfers between devices with their start and end apart: 3, of which 2 were waited for; matrix products, arithmetic and copies ran while one was open for 1% of the time, Pallas kernels for 0%

commit v1 on v0

v1 whole, which is shorter than its diff:
```python
import jax
import jax.numpy as jnp
from jax import lax
from jax.sharding import Mesh, PartitionSpec as P

F32 = jnp.float32
BF16 = jnp.bfloat16
VERTEX = ("x", "z", "c")


def shards(node_feats, adj_tiles, tile_cols, degrees, w_self, w_neigh, hidden_bias, cotangent):
    node_count, feat_local = node_feats.shape
    blk_here, _, tile_size, _ = adj_tiles.shape
    vertex_count = lax.axis_size(VERTEX)
    feat_count = lax.axis_size("feat")
    rows_own = node_count // feat_count
    hidden_units = w_self.shape[1]

    forward = [(i, (i + 1) % vertex_count) for i in range(vertex_count)]
    backward = [(target, source) for source, target in forward]
    low = lax.ppermute(node_feats, VERTEX, forward)
    high = lax.ppermute(node_feats, VERTEX, backward)
    blocks = jnp.concatenate([low, node_feats, high], axis=0)
    blocks = blocks.reshape(3 * blk_here, tile_size, feat_local)
    vertex_idx = lax.axis_index(VERTEX)
    local_cols = (tile_cols - vertex_idx * blk_here + blk_here) % (blk_here * vertex_count)
    picked = blocks[local_cols]
    summed = jnp.einsum("bkij,bkjf->bif", adj_tiles, picked, preferred_element_type=F32)
    summed = summed.reshape(node_count, feat_local)
    averaged = (summed / degrees.astype(F32)[:, None]).astype(BF16)

    rows = jnp.concatenate([node_feats, averaged], axis=1).T
    rows = rows.reshape(2 * feat_local, feat_count, rows_own).transpose(1, 0, 2)
    weights = jnp.concatenate([w_self, w_neigh], axis=0)
    half = hidden_units // 2
    weights = jnp.concatenate([weights[:, :half], weights[:, half:]], axis=0)
    packed = jnp.concatenate(
        [rows, jnp.broadcast_to(weights[None], (feat_count,) + weights.shape)], axis=1
    )
    packed = lax.all_to_all(packed, "feat", 0, 0, tiled=True)
    width = 2 * feat_local
    inputs = packed[:, :width].reshape(feat_count * width, rows_own)
    weights = jnp.concatenate([packed[:, width : 2 * width], packed[:, 2 * width :]], axis=2)
    weights = weights.reshape(feat_count * width, hidden_units)

    preact = (
        lax.dot_general(inputs, weights, (((0,), (0,)), ((), ())), preferred_element_type=F32)
        + hidden_bias
    )
    hidden = jnp.maximum(preact, 0.0).astype(BF16)
    grad_pre = jnp.where(preact > 0, cotangent, jnp.zeros_like(cotangent))
    grads = jnp.dot(inputs, grad_pre, preferred_element_type=F32)
    grads = grads.reshape(feat_count, width, hidden_units)
    bias_row = jnp.sum(grad_pre.astype(F32), axis=0)
    bias_row = jnp.broadcast_to(bias_row, (feat_count, 8, hidden_units))
    grads = jnp.concatenate([grads, bias_row], axis=1)

    grads = lax.all_to_all(grads, "feat", 0, 0, tiled=True).sum(0)
    grads = lax.all_gather(grads, ("x", "c")).sum(0)
    grads = lax.all_gather(grads, "z").sum(0)
    return (hidden, grads[:feat_local], grads[feat_local:width], grads[width])


def solution(mesh):
    sizes = {"x": 4, "z": 8, "c": 2, "feat": 8}
    grid = Mesh(mesh.devices.reshape(tuple(sizes.values())), tuple(sizes))
    return jax.shard_map(
        shards,
        mesh=grid,
        in_specs=(
            P(VERTEX, "feat"),
            P(VERTEX, None, None, None),
            P(VERTEX, None),
            P(VERTEX),
            P("feat", None),
            P("feat", None),
            P(),
            P((*VERTEX, "feat"), None),
        ),
        out_specs=(P((*VERTEX, "feat"), None), P("feat", None), P("feat", None), P()),
        check_vma=False,
    )
```

time: 349 us -> 94.3 us (0.27)
  the two profiles are of different devices: /device:TPU:1 before, /device:TPU:8 now
where the time goes in v1:
time: 94.3 us; the launch traced here: 93.8 us
  blocking collectives  67 us (71%)
  starting transfers between devices  14.6 us (15%)
  waiting for transfers between devices  3.94 us (4%)
  local copies, waits for them, and re-layouts  3.51 us (4%)
  other arithmetic  2.37 us (3%)
  matrix products  1.51 us (2%)
    all_gather x1, blocking collectives, shards(): grads = lax.all_gather(grads, 'z').sum(0)  24.9 us
    all_to_all x1, blocking collectives, shards(): packed = lax.all_to_all(packed, 'feat', 0, 0, tiled=True)  15.7 us
    all_to_all x1, blocking collectives, shards(): grads = lax.all_to_all(grads, 'feat', 0, 0, tiled=True).sum(0)  13.6 us
    all_gather x1, blocking collectives, shards(): grads = lax.all_gather(grads, ('x', 'c')).sum(0)  12.9 us
    ppermute x1, starting transfers between devices, shards(): high = lax.ppermute(node_feats, VERTEX, backward)  12.7 us
    ppermute x1, waiting for transfers between devices, shards(): low = lax.ppermute(node_feats, VERTEX, forward)  3.93 us
    ppermute x1, starting transfers between devices, shards(): low = lax.ppermute(node_feats, VERTEX, forward)  1.92 us
  transfers between devices with their start and end apart: 2, of which 1 were waited for; matrix products, arithmetic and copies ran while one was open for 3% of the time, Pallas kernels for 0%

profile of v1, /device:TPU:8, one launch (start us, length us, event | category | flops | bytes accessed | tf_op | source)
XLA Modules:
  0.0 93.8 jit_solution(15087542746254509739)
XLA Ops:
  0.6 0.0 copy-start
  0.6 12.7 %collective-permute-start.1 = (bf16[1024,16]{0,1:T(8,128)(2,1)}, bf16[1024,16]{0,1:T(8,128)(2,1)S(1)}, u32[]{:S(2)}, u32[]{:S(2)}) collective-permute-start(bf16[1024,16]{0,1:T(8,128)(2,1)} %param.8), channel_id=1, source_target_pairs={{8,0},{16,8},{24,16},{32,24},{40,32},{48,40},{56,48},{64,56},{72,6... | collective-permute-start | bytes 98312 | tf_op jit(solution)/shard_map/ppermute | solution.py:22
  13.4 1.9 %collective-permute-start = (bf16[1024,16]{0,1:T(8,128)(2,1)}, bf16[1024,16]{0,1:T(8,128)(2,1)S(1)}, u32[]{:S(2)}, u32[]{:S(2)}) collective-permute-start(bf16[1024,16]{0,1:T(8,128)(2,1)} %param.8), channel_id=1, source_target_pairs={{0,8},{8,16},{16,24},{24,32},{32,40},{40,48},{48,56},{56,64},{64,7... | collective-permute-start | bytes 98312 | tf_op jit(solution)/shard_map/ppermute | solution.py:21
  15.3 0.7 compare_select_fusion.1
  16.0 0.1 reshape.30
  16.1 0.7 constant_dynamic-update-slice_fusion.1
  16.8 0.7 constant_dynamic-update-slice_fusion
  17.5 0.7 convert_element_type.12
  18.2 0.0 collective-permute-done.1
  18.2 3.9 %collective-permute-done = bf16[1024,16]{0,1:T(8,128)(2,1)S(1)} collective-permute-done((bf16[1024,16]{0,1:T(8,128)(2,1)}, bf16[1024,16]{0,1:T(8,128)(2,1)S(1)}, u32[]{:S(2)}, u32[]{:S(2)}) %collective-permute-start) | collective-permute-done | bytes 32800 | tf_op jit(solution)/shard_map/ppermute | solution.py:21
  22.1 0.8 copy_bitcast_fusion
  22.9 0.6 gather_fusion
  23.5 0.0 copy-start.2
  23.5 0.0 copy-done
  23.6 0.0 copy-start.3
  23.6 0.0 copy-start.1
  23.6 0.5 convolution_bitcast_fusion.1
  24.1 0.2 copy-done.2
  24.4 15.7 %all_to_all.10 = bf16[8,96,128]{2,1,0:T(8,128)(2,1)S(1)} all-to-all(bf16[8,96,128]{2,1,0:T(8,128)(2,1)S(1)} %pad_maximum_fusion.1), channel_id=1, replica_groups=mesh['x'=4,'z'=8,'c'=2,'feat'=8] {'feat'}, dimensions={0} | all-to-all | bytes 393216 | tf_op jit(solution)/shard_map/all_to_all | solution.py:40
  40.0 0.0 copy-done.3
  40.0 0.8 maximum_convert_fusion
  40.9 0.0 copy-done.1
  40.9 0.2 fusion.5
  41.2 13.6 %all_to_all.11 = f32[8,40,256]{2,1,0:T(8,128)S(1)} all-to-all(f32[8,40,256]{2,1,0:T(8,128)S(1)} %pad_maximum_fusion), channel_id=1, replica_groups=mesh['x'=4,'z'=8,'c'=2,'feat'=8] {'feat'}, dimensions={0} | all-to-all | bytes 655360 | tf_op jit(solution)/shard_map/all_to_all | solution.py:58
  54.7 12.9 %all-gather = f32[320,256]{1,0:T(8,128)S(1)} all-gather(f32[40,256]{1,0:T(8,128)S(1)} %reduce_sum.37), channel_id=2, replica_groups=mesh['x'=4,'z'=8,'c'=2,'feat'=8] {'x','c'}, dimensions={0}, use_global_device_ids=true | all-gather | bytes 368640 | tf_op jit(solution)/shard_map/all_gather | solution.py:59
  67.7 24.9 %all-gather.1 = f32[320,256]{1,0:T(8,128)S(1)} all-gather(f32[40,256]{1,0:T(8,128)S(1)} %reduce_sum.38), channel_id=3, replica_groups=mesh['x'=4,'z'=8,'c'=2,'feat'=8] {'z'}, dimensions={0}, use_global_device_ids=true | all-gather | bytes 368640 | tf_op jit(solution)/shard_map/all_gather | solution.py:60
  92.6 0.6 slice.41
  93.2 0.6 fusion.12
  (14 shorter events, 0.2 us)
Async XLA Ops:
  0.6 22.9 %copy-start = (bf16[8,6,128,128]{3,2,1,0:T(8,128)(2,1)S(1)}, bf16[8,6,128,128]{3,2,1,0:T(8,128)(2,1)}, u32[]{:S(2)}) copy-start(bf16[8,6,128,128]{3,2,1,0:T(8,128)(2,1)} %param.9) | copy-start | bytes 4718596
  0.6 17.6 %collective-permute-start.1 = (bf16[1024,16]{0,1:T(8,128)(2,1)}, bf16[1024,16]{0,1:T(8,128)(2,1)S(1)}, u32[]{:S(2)}, u32[]{:S(2)}) collective-permute-start(bf16[1024,16]{0,1:T(8,128)(2,1)} %param.8), channel_id=1, source_target_pairs={{8,0},{16,8},{24,16},{32,24},{40,32},{48,40},{56,48},{64,56},{72,6... | collective-permute-start | bytes 98312 | tf_op jit(solution)/shard_map/ppermute | solution.py:22
  13.4 8.8 %collective-permute-start = (bf16[1024,16]{0,1:T(8,128)(2,1)}, bf16[1024,16]{0,1:T(8,128)(2,1)S(1)}, u32[]{:S(2)}, u32[]{:S(2)}) collective-permute-start(bf16[1024,16]{0,1:T(8,128)(2,1)} %param.8), channel_id=1, source_target_pairs={{0,8},{8,16},{16,24},{24,32},{32,40},{40,48},{48,56},{56,64},{64,7... | collective-permute-start | bytes 98312 | tf_op jit(solution)/shard_map/ppermute | solution.py:21
  23.5 0.8 copy-start.2
  23.6 16.5 %copy-start.3 = (f32[256]{0:T(256)S(1)}, f32[256]{0:T(256)}, u32[]{:S(2)}) copy-start(f32[256]{0:T(256)} %param.14) | copy-start | bytes 3076
  23.6 17.3 %copy-start.1 = (bf16[128,256]{1,0:T(8,128)(2,1)S(1)}, bf16[128,256]{1,0:T(8,128)(2,1)}, u32[]{:S(2)}) copy-start(bf16[128,256]{1,0:T(8,128)(2,1)} %param.15) | copy-start | bytes 196612

commit v2 on v1

v2 whole, which is shorter than its diff:
```python
import functools

import jax
import jax.numpy as jnp
from jax import lax
from jax.experimental import pallas as pl
from jax.experimental.pallas import tpu as pltpu
from jax.sharding import Mesh, PartitionSpec as P

F32 = jnp.float32
BF16 = jnp.bfloat16
VERTEX = ("x", "z", "c")
NT = (((1,), (1,)), ((), ()))
TN = (((0,), (0,)), ((), ()))
VMEM = pl.BlockSpec(memory_space=pltpu.VMEM)
SMEM = pl.BlockSpec(memory_space=pltpu.SMEM)


def call(kernel, out_shape, in_specs, scratch_shapes=(), flops=0):
    many = isinstance(out_shape, (tuple, list))
    return pl.pallas_call(
        kernel,
        out_shape=out_shape,
        in_specs=in_specs,
        out_specs=[VMEM] * len(out_shape) if many else VMEM,
        scratch_shapes=list(scratch_shapes),
        compiler_params=pltpu.CompilerParams(vmem_limit_bytes=32 * 1024 * 1024),
        cost_estimate=pl.CostEstimate(flops=flops, bytes_accessed=2000000, transcendentals=0),
    )


def aggregate_kernel(
    total_blocks, cols_ref, place_ref, pair_ref, far_ref, own_ref, adj_ref, deg_ref, ws_ref, wn_ref, out_ref, feats
):
    blocks, tiles, _, size = adj_ref.shape
    width = own_ref.shape[0]
    half = ws_ref.shape[1] // 2
    for b in range(blocks):
        feats[b] = pair_ref[0, :, b * size : (b + 1) * size]
        feats[blocks + b] = pair_ref[1, :, b * size : (b + 1) * size]
        feats[2 * blocks + b] = far_ref[:, b * size : (b + 1) * size]
    first = place_ref[0]
    turn = place_ref[1]
    for r in range(blocks):
        total = jnp.zeros((width, size), F32)
        for k in range(tiles):
            col = lax.rem(cols_ref[r, k] - first + blocks + total_blocks, total_blocks)
            spot = lax.rem(col + turn, 3 * blocks)
            total += lax.dot_general(feats[spot], adj_ref[r, k], NT, preferred_element_type=F32)
        degree = deg_ref[:, r * size : (r + 1) * size].astype(F32)
        out_ref[r, :width] = own_ref[:, r * size : (r + 1) * size]
        out_ref[r, width : 2 * width] = (total / degree).astype(BF16)
        for h in range(2):
            at = 2 * width * (1 + h)
            out_ref[r, at : at + width] = ws_ref[:, h * half : (h + 1) * half]
            out_ref[r, at + width : at + 2 * width] = wn_ref[:, h * half : (h + 1) * half]


def layer_kernel(width, packed_ref, cot_ref, bias_ref, hidden_ref, grads_ref):
    feat_count = packed_ref.shape[0]
    rows = packed_ref.shape[2]
    half = rows
    inputs = packed_ref[:, : 2 * width].reshape(feat_count * 2 * width, rows)
    left = packed_ref[:, 2 * width : 4 * width].reshape(feat_count * 2 * width, half)
    right = packed_ref[:, 4 * width : 6 * width].reshape(feat_count * 2 * width, half)
    ones = jnp.ones((16, rows), BF16)
    for h, weights in enumerate((left, right)):
        lanes = slice(h * half, (h + 1) * half)
        preact = lax.dot_general(inputs, weights, TN, preferred_element_type=F32) + bias_ref[:, lanes]
        hidden_ref[:, lanes] = jnp.maximum(preact, 0.0).astype(BF16)
        cot = cot_ref[:, lanes].astype(F32)
        grad_pre = jnp.where(preact > 0, cot, 0.0).astype(BF16)
        grads = jnp.dot(inputs, grad_pre, preferred_element_type=F32)
        grads = grads.reshape(feat_count, 2, width, half)
        bias = jnp.dot(ones, grad_pre, preferred_element_type=F32).astype(grads_ref.dtype)
        for c in range(2):
            for f in range(feat_count):
                grads_ref[c, f, h * width : (h + 1) * width] = grads[f, c].astype(grads_ref.dtype)
                if c == h:
                    grads_ref[c, f, 2 * width :] = bias


def sum_kernel(rows_ref, out_ref):
    total = rows_ref[0].astype(F32)
    for i in range(1, rows_ref.shape[0]):
        total += rows_ref[i].astype(F32)
    if len(out_ref.shape) == 2:
        out_ref[...] = total.astype(out_ref.dtype)
    else:
        total = total.astype(out_ref.dtype)
        for i in range(out_ref.shape[0]):
            out_ref[i] = total


def unpack_kernel(width, pair_ref, self_ref, neigh_ref, bias_ref):
    half = pair_ref.shape[2]
    for h in range(2):
        lanes = slice(h * half, (h + 1) * half)
        self_ref[:, lanes] = pair_ref[0, h * width : (h + 1) * width]
        neigh_ref[:, lanes] = pair_ref[1, h * width : (h + 1) * width]
        bias_ref[:, lanes] = pair_ref[h, 2 * width : 2 * width + 1]


def shards(node_feats, adj_tiles, tile_cols, degrees, w_self, w_neigh, hidden_bias, cotangent):
    node_count, width = node_feats.shape
    blocks, tiles, size, _ = adj_tiles.shape
    vertex_count = lax.axis_size(VERTEX)
    feat_count = lax.axis_size("feat")
    chip_count = vertex_count // 2
    rows_own = node_count // feat_count
    hidden_units = w_self.shape[1]

    feats = node_feats.T
    away = [(v, (v - 1 if v % 2 == 0 else v + 1) % vertex_count) for v in range(vertex_count)]
    far = lax.ppermute(feats, VERTEX, away)
    pair = lax.all_gather(feats, "c")
    vertex_idx = lax.axis_index(VERTEX)
    core = lax.axis_index("c")
    place = jnp.stack([vertex_idx * blocks, (1 - core) * (2 * blocks)]).astype(jnp.int32)
    packed = call(
        functools.partial(aggregate_kernel, blocks * vertex_count),
        jax.ShapeDtypeStruct((feat_count, 6 * width, rows_own), BF16),
        [SMEM, SMEM] + [VMEM] * 7,
        [pltpu.VMEM((3 * blocks, width, size), BF16)],
        flops=2 * blocks * tiles * size * size * width,
    )(tile_cols, place, pair, far, feats, adj_tiles, degrees.reshape(1, -1), w_self, w_neigh)

    packed = lax.all_to_all(packed, "feat", 0, 0, tiled=True)
    hidden, grads = call(
        functools.partial(layer_kernel, width),
        (
            jax.ShapeDtypeStruct((rows_own, hidden_units), BF16),
            jax.ShapeDtypeStruct((2, feat_count, 3 * width, rows_own), BF16),
        ),
        [VMEM] * 3,
        flops=4 * rows_own * 256 * hidden_units,
    )(packed, cotangent, hidden_bias.reshape(1, -1))

    grads = lax.all_to_all(
        grads.reshape(2 * feat_count, 3 * width, rows_own), ("c", "feat"), 0, 0, tiled=True
    )
    grads = call(
        sum_kernel, jax.ShapeDtypeStruct((chip_count, 3 * width, rows_own), BF16), [VMEM]
    )(grads)
    grads = lax.all_to_all(grads, ("x", "z"), 0, 0, tiled=True)
    grads = call(sum_kernel, jax.ShapeDtypeStruct((3 * width, rows_own), F32), [VMEM])(grads)
    pair = lax.all_gather(grads, "c")
    grad_self, grad_neigh, grad_bias = call(
        functools.partial(unpack_kernel, width),
        (
            jax.ShapeDtypeStruct((width, hidden_units), F32),
            jax.ShapeDtypeStruct((width, hidden_units), F32),
            jax.ShapeDtypeStruct((1, hidden_units), F32),
        ),
        [VMEM],
    )(pair)
    return (hidden, grad_self, grad_neigh, grad_bias.reshape(hidden_units))


def solution(mesh):
    sizes = {"x": 4, "z": 8, "c": 2, "feat": 8}
    grid = Mesh(mesh.devices.reshape(tuple(sizes.values())), tuple(sizes))
    return jax.shard_map(
        shards,
        mesh=grid,
        in_specs=(
            P(VERTEX, "feat"),
            P(VERTEX, None, None, None),
            P(VERTEX, None),
            P(VERTEX),
            P("feat", None),
            P("feat", None),
            P(),
            P((*VERTEX, "feat"), None),
        ),
        out_specs=(P((*VERTEX, "feat"), None), P("feat", None), P("feat", None), P()),
        check_vma=False,
    )
```

time: 94.3 us -> 74.8 us (0.79)
  the two profiles are of different devices: /device:TPU:8 before, /device:TPU:1 now
where the time goes in v2:
time: 74.8 us; the launch traced here: 74.3 us
  blocking collectives  59.8 us (80%)
  starting transfers between devices  5.52 us (7%)
  local copies, waits for them, and re-layouts  4.94 us (7%)
  Pallas kernels  3.27 us (4%)
    all_to_all x1, blocking collectives, shards(): packed = lax.all_to_all(packed, 'feat', 0, 0, tiled=True)  16.1 us
    all_to_all x1, blocking collectives, shards(): grads = lax.all_to_all(grads, ('x', 'z'), 0, 0, tiled=True)  14.5 us
    all_to_all x1, blocking collectives, shards(): lax.all_to_all(grads.reshape(2 * feat_count, 3 * width, rows_own), ('c',...  12.7 us
    all_gather x1, blocking collectives, shards(): pair = lax.all_gather(feats, 'c')  10.4 us
    all_gather x1, blocking collectives, shards(): pair = lax.all_gather(grads, 'c')  6.09 us
    ppermute x1, starting transfers between devices, shards(): far = lax.ppermute(feats, VERTEX, away)  5.52 us
    unnamed x16, local copies, waits for them, and re-layouts  4.94 us
    pallas_call x1, Pallas kernels, shards(): call(functools.partial(aggregate_kernel, blocks * vertex_count), jax.Shap...  1.52 us
  transfers between devices with their start and end apart: 1, of which 0 were waited for; matrix products, arithmetic and copies ran while one was open for 0% of the time, Pallas kernels for 0%

profile of v2, /device:TPU:1, one launch (start us, length us, event | category | flops | bytes accessed | tf_op | source)
XLA Modules:
  0.0 74.3 jit_solution(15655828564121524677)
XLA Ops:
  0.6 0.0 copy-start.2
  0.6 0.0 copy-start.7
  0.7 5.5 %collective-permute-start = (bf16[16,1024]{1,0:T(8,128)(2,1)}, bf16[16,1024]{1,0:T(8,128)(2,1)S(1)}, u32[]{:S(2)}, u32[]{:S(2)}) collective-permute-start(bf16[16,1024]{1,0:T(8,128)(2,1)} %bitcast.12), channel_id=1, source_target_pairs={{0,504},{8,16},{16,8},{24,32},{32,24},{40,48},{48,40},{56,64},{64,... | collective-permute-start | bytes 98312 | tf_op jit(solution)/shard_map/ppermute | solution.py:115
  6.2 0.1 pad_add_fusion.place_ref
  6.3 10.4 %all-gather = bf16[32,1024]{1,0:T(8,128)(2,1)S(1)} all-gather(bf16[16,1024]{1,0:T(8,128)(2,1)} %bitcast.13), channel_id=2, replica_groups=mesh['x'=4,'z'=8,'c'=2,'feat'=8] {'c'}, dimensions={0}, use_global_device_ids=true | all-gather | bytes 98304 | tf_op jit(solution)/shard_map/all_gather | solution.py:116
  16.7 0.0 collective-permute-done.far_ref
  16.7 0.0 copy-start
  16.7 1.4 %copy-done = bf16[8,6,128,128]{3,2,1,0:T(8,128)(2,1)S(1)} copy-done((bf16[8,6,128,128]{3,2,1,0:T(8,128)(2,1)S(1)}, bf16[8,6,128,128]{3,2,1,0:T(8,128)(2,1)}, u32[]{:S(2)}) %copy-start) | copy-done | bytes 1572888
  18.1 0.0 copy-start.1
  18.1 0.8 %copy-done.1 = bf16[1024,16]{0,1:T(8,128)(2,1)S(1)} copy-done((bf16[1024,16]{0,1:T(8,128)(2,1)S(1)}, bf16[1024,16]{0,1:T(8,128)(2,1)}, u32[]{:S(2)}) %copy-start.1) | copy-done | bytes 32792
  18.8 0.0 copy-start.3
  18.8 0.7 copy-done.3
  19.5 0.0 copy-start.4
  19.5 0.7 copy-done.4
  20.2 0.0 copy-start.5
  20.2 0.7 copy-done.5
  20.9 0.0 copy-start.6
  20.9 0.7 copy-done.6
  21.6 1.5 %shard_map.111 = bf16[8,96,128]{2,1,0:T(8,128)(2,1)S(1)} custom-call(s32[8,6]{1,0:T(8,128)S(1)} %copy-done.5, s32[2]{0:T(128)S(1)} %pad_add_fusion.place_ref, bf16[2,16,1024]{2,1,0:T(8,128)(2,1)S(1)} %bitcast.9, bf16[16,1024]{1,0:T(8,128)(2,1)S(1)} %collective-permute-done.far_ref, bf16[16,1024]{1,0:T(8,128)(2,1)S(1)} %bitcast.14, ...), custom_call_target="tpu_custom_call" | custom-call | flops 25165824 | bytes 2000000 | tf_op jit(solution)/shard_map/pallas_call | solution.py:120
  23.1 16.1 %all_to_all.15.packed_ref = bf16[8,96,128]{2,1,0:T(8,128)(2,1)S(1)} all-to-all(bf16[8,96,128]{2,1,0:T(8,128)(2,1)S(1)} %shard_map.111), channel_id=1, replica_groups=mesh['x'=4,'z'=8,'c'=2,'feat'=8] {'feat'}, dimensions={0} | all-to-all | bytes 393216 | tf_op jit(solution)/shard_map/all_to_all | solution.py:128
  39.2 0.0 copy-done.2
  39.2 0.0 copy-done.7
  39.2 1.0 %shard_map.112 = (bf16[128,256]{1,0:T(8,128)(2,1)}, bf16[2,8,48,128]{3,2,1,0:T(8,128)(2,1)S(1)}) custom-call(bf16[8,96,128]{2,1,0:T(8,128)(2,1)S(1)} %all_to_all.15.packed_ref, bf16[128,256]{1,0:T(8,128)(2,1)S(1)} %copy-done.2, f32[1,256]{1,0:T(1,128)S(1)} %bitcast.16), custom_call_target="tpu_custom_call" | custom-call | flops 33554432 | bytes 2000000 | tf_op jit(solution)/shard_map/pallas_call | solution.py:129
  40.2 12.7 %all_to_all.16.rows_ref = bf16[16,48,128]{2,1,0:T(8,128)(2,1)S(1)} all-to-all(bf16[16,48,128]{2,1,0:T(8,128)(2,1)S(1)} %bitcast.10), channel_id=1, replica_groups=mesh['x'=4,'z'=8,'c'=2,'feat'=8] {'c','feat'}, dimensions={0} | all-to-all | bytes 393216 | tf_op jit(solution)/shard_map/all_to_all | solution.py:139
  53.0 14.5 %all_to_all.17.rows_ref = bf16[32,48,128]{2,1,0:T(8,128)(2,1)S(1)} all-to-all(bf16[32,48,128]{2,1,0:T(8,128)(2,1)S(1)} %shard_map.113), channel_id=1, replica_groups=mesh['x'=4,'z'=8,'c'=2,'feat'=8] {'x','z'}, dimensions={0} | all-to-all | bytes 786432 | tf_op jit(solution)/shard_map/all_to_all | solution.py:145
  67.5 0.1 shard_map.114
  67.6 6.1 %all-gather.1 = f32[96,128]{1,0:T(8,128)S(1)} all-gather(f32[48,128]{1,0:T(8,128)S(1)} %shard_map.114), channel_id=3, replica_groups=mesh['x'=4,'z'=8,'c'=2,'feat'=8] {'c'}, dimensions={0}, use_global_device_ids=true | all-gather | bytes 73728 | tf_op jit(solution)/shard_map/all_gather | solution.py:147
  73.7 0.6 shard_map.115
  (1 shorter events, 0.0 us)
Async XLA Ops:
  0.6 38.6 %copy-start.2 = (bf16[128,256]{1,0:T(8,128)(2,1)S(1)}, bf16[128,256]{1,0:T(8,128)(2,1)}, u32[]{:S(2)}) copy-start(bf16[128,256]{1,0:T(8,128)(2,1)} %cot_ref.1) | copy-start | bytes 196612
  0.6 38.6 %copy-start.7 = (f32[256]{0:T(256)S(1)}, f32[256]{0:T(256)}, u32[]{:S(2)}) copy-start(f32[256]{0:T(256)} %param.14) | copy-start | bytes 3076
  0.7 16.0 %collective-permute-start = (bf16[16,1024]{1,0:T(8,128)(2,1)}, bf16[16,1024]{1,0:T(8,128)(2,1)S(1)}, u32[]{:S(2)}, u32[]{:S(2)}) collective-permute-start(bf16[16,1024]{1,0:T(8,128)(2,1)} %bitcast.12), channel_id=1, source_target_pairs={{0,504},{8,16},{16,8},{24,32},{32,24},{40,48},{48,40},{56,64},{64,... | collective-permute-start | bytes 98312 | tf_op jit(solution)/shard_map/ppermute | solution.py:115
  16.7 1.4 %copy-start = (bf16[8,6,128,128]{3,2,1,0:T(8,128)(2,1)S(1)}, bf16[8,6,128,128]{3,2,1,0:T(8,128)(2,1)}, u32[]{:S(2)}) copy-start(bf16[8,6,128,128]{3,2,1,0:T(8,128)(2,1)} %adj_ref.1) | copy-start | bytes 4718596
  18.1 0.8 %copy-start.1 = (bf16[1024,16]{0,1:T(8,128)(2,1)S(1)}, bf16[1024,16]{0,1:T(8,128)(2,1)}, u32[]{:S(2)}) copy-start(bf16[1024,16]{0,1:T(8,128)(2,1)} %param.8) | copy-start | bytes 98308
  18.8 0.7 copy-start.3
  19.5 0.7 copy-start.4
  20.2 0.7 copy-start.5
  20.9 0.7 copy-start.6

commit v3 on v2

--- a/solution.py
+++ b/solution.py
@@ -16,22 +16,34 @@
 SMEM = pl.BlockSpec(memory_space=pltpu.SMEM)
 
 
-def call(kernel, out_shape, in_specs, scratch_shapes=(), flops=0):
-    many = isinstance(out_shape, (tuple, list))
+def call(kernel, out_shape, in_specs, scratch_shapes=(), flops=0, out_specs=None):
+    if out_specs is None:
+        out_specs = [VMEM] * len(out_shape) if isinstance(out_shape, tuple) else VMEM
     return pl.pallas_call(
         kernel,
         out_shape=out_shape,
         in_specs=in_specs,
-        out_specs=[VMEM] * len(out_shape) if many else VMEM,
+        out_specs=out_specs,
         scratch_shapes=list(scratch_shapes),
         compiler_params=pltpu.CompilerParams(vmem_limit_bytes=32 * 1024 * 1024),
         cost_estimate=pl.CostEstimate(flops=flops, bytes_accessed=2000000, transcendentals=0),
     )
 
 
-def aggregate_kernel(
-    total_blocks, cols_ref, place_ref, pair_ref, far_ref, own_ref, adj_ref, deg_ref, ws_ref, wn_ref, out_ref, feats
-):
+def places_kernel(total_blocks, cols_ref, place_ref, spots_ref):
+    blocks, tiles = cols_ref.shape
+    first = place_ref[0]
+    turn = place_ref[1]
+    for r in range(blocks):
+        for k in range(tiles):
+            col = cols_ref[r, k] - first + blocks
+            col = jnp.where(col < 0, col + total_blocks, col)
+            col = jnp.where(col >= total_blocks, col - total_blocks, col)
+            spot = col + turn
+            spots_ref[r, k] = jnp.where(spot >= 3 * blocks, spot - 3 * blocks, spot)
+
+
+def aggregate_kernel(spots_ref, pair_ref, far_ref, own_ref, adj_ref, deg_ref, ws_ref, wn_ref, out_ref, feats):
     blocks, tiles, _, size = adj_ref.shape
     width = own_ref.shape[0]
     half = ws_ref.shape[1] // 2
@@ -39,14 +51,10 @@
         feats[b] = pair_ref[0, :, b * size : (b + 1) * size]
         feats[blocks + b] = pair_ref[1, :, b * size : (b + 1) * size]
         feats[2 * blocks + b] = far_ref[:, b * size : (b + 1) * size]
-    first = place_ref[0]
-    turn = place_ref[1]
     for r in range(blocks):
-        total = jnp.zeros((width, size), F32)
-        for k in range(tiles):
-            col = lax.rem(cols_ref[r, k] - first + blocks + total_blocks, total_blocks)
-            spot = lax.rem(col + turn, 3 * blocks)
-            total += lax.dot_general(feats[spot], adj_ref[r, k], NT, preferred_element_type=F32)
+        picked = jnp.concatenate([feats[spots_ref[r, k]] for k in range(tiles)], axis=1)
+        weights = jnp.concatenate([adj_ref[r, k] for k in range(tiles)], axis=1)
+        total = lax.dot_general(picked, weights, NT, preferred_element_type=F32)
         degree = deg_ref[:, r * size : (r + 1) * size].astype(F32)
         out_ref[r, :width] = own_ref[:, r * size : (r + 1) * size]
         out_ref[r, width : 2 * width] = (total / degree).astype(BF16)
@@ -63,7 +71,7 @@
     inputs = packed_ref[:, : 2 * width].reshape(feat_count * 2 * width, rows)
     left = packed_ref[:, 2 * width : 4 * width].reshape(feat_count * 2 * width, half)
     right = packed_ref[:, 4 * width : 6 * width].reshape(feat_count * 2 * width, half)
-    ones = jnp.ones((16, rows), BF16)
+    ones = jnp.ones((8, rows), BF16)
     for h, weights in enumerate((left, right)):
         lanes = slice(h * half, (h + 1) * half)
         preact = lax.dot_general(inputs, weights, TN, preferred_element_type=F32) + bias_ref[:, lanes]
@@ -92,7 +100,8 @@
             out_ref[i] = total
 
 
-def unpack_kernel(width, pair_ref, self_ref, neigh_ref, bias_ref):
+def unpack_kernel(width, pair_ref, layer_ref, hidden_ref, self_ref, neigh_ref, bias_ref):
+    hidden_ref[...] = layer_ref[...]
     half = pair_ref.shape[2]
     for h in range(2):
         lanes = slice(h * half, (h + 1) * half)
@@ -117,43 +126,51 @@
     vertex_idx = lax.axis_index(VERTEX)
     core = lax.axis_index("c")
     place = jnp.stack([vertex_idx * blocks, (1 - core) * (2 * blocks)]).astype(jnp.int32)
+    spots = call(
+        functools.partial(places_kernel, blocks * vertex_count),
+        jax.ShapeDtypeStruct((blocks, tiles), jnp.int32),
+        [SMEM] * 2,
+        flops=5 * 10**9,
+        out_specs=SMEM,
+    )(tile_cols, place)
     packed = call(
-        functools.partial(aggregate_kernel, blocks * vertex_count),
+        aggregate_kernel,
         jax.ShapeDtypeStruct((feat_count, 6 * width, rows_own), BF16),
-        [SMEM, SMEM] + [VMEM] * 7,
+        [SMEM] + [VMEM] * 7,
         [pltpu.VMEM((3 * blocks, width, size), BF16)],
         flops=2 * blocks * tiles * size * size * width,
-    )(tile_cols, place, pair, far, feats, adj_tiles, degrees.reshape(1, -1), w_self, w_neigh)
+    )(spots, pair, far, feats, adj_tiles, degrees.reshape(1, -1), w_self, w_neigh)
 
     packed = lax.all_to_all(packed, "feat", 0, 0, tiled=True)
     hidden, grads = call(
         functools.partial(layer_kernel, width),
         (
             jax.ShapeDtypeStruct((rows_own, hidden_units), BF16),
-            jax.ShapeDtypeStruct((2, feat_count, 3 * width, rows_own), BF16),
+            jax.ShapeDtypeStruct((2, feat_count, 2 * width + 8, rows_own), BF16),
         ),
         [VMEM] * 3,
         flops=4 * rows_own * 256 * hidden_units,
     )(packed, cotangent, hidden_bias.reshape(1, -1))
 
     grads = lax.all_to_all(
-        grads.reshape(2 * feat_count, 3 * width, rows_own), ("c", "feat"), 0, 0, tiled=True
+        grads.reshape(2 * feat_count, 2 * width + 8, rows_own), ("c", "feat"), 0, 0, tiled=True
     )
     grads = call(
-        sum_kernel, jax.ShapeDtypeStruct((chip_count, 3 * width, rows_own), BF16), [VMEM]
+        sum_kernel, jax.ShapeDtypeStruct((chip_count, 2 * width + 8, rows_own), BF16), [VMEM]
     )(grads)
     grads = lax.all_to_all(grads, ("x", "z"), 0, 0, tiled=True)
-    grads = call(sum_kernel, jax.ShapeDtypeStruct((3 * width, rows_own), F32), [VMEM])(grads)
+    grads = call(sum_kernel, jax.ShapeDtypeStruct((2 * width + 8, rows_own), F32), [VMEM])(grads)
     pair = lax.all_gather(grads, "c")
-    grad_self, grad_neigh, grad_bias = call(
+    hidden, grad_self, grad_neigh, grad_bias = call(
         functools.partial(unpack_kernel, width),
         (
+            jax.ShapeDtypeStruct((rows_own, hidden_units), BF16),
             jax.ShapeDtypeStruct((width, hidden_units), F32),
             jax.ShapeDtypeStruct((width, hidden_units), F32),
             jax.ShapeDtypeStruct((1, hidden_units), F32),
         ),
-        [VMEM],
-    )(pair)
+        [VMEM] * 2,
+    )(pair, hidden)
     return (hidden, grad_self, grad_neigh, grad_bias.reshape(hidden_units))
 
 

time: 74.8 us -> 69.1 us (0.924)
  local copies, waits for them, and re-layouts: 4.94 us -> 0.72 us
  blocking collectives: 59.8 us -> 58 us
    unnamed x16, local copies, waits for them, and re-layouts: 4.94 us -> 0.72 us
    all_to_all x1, blocking collectives: 14.5 us -> 13.4 us  [shards(): grads = lax.all_to_all(grads, ('x', 'z'), 0, 0, tiled=True)]
    pallas_call x4 -> x5, Pallas kernels: 2.25 us -> 3.29 us  [the longest x1 1.43 us: shards(): call(functools.partial(places_kernel, blocks * vertex_count), jax.ShapeDt...]
  transfers between devices with their start and end apart: 1 -> 1, of which waited for: 0 -> 0; matrix products, arithmetic and copies ran while one was open for 0% -> 0% of each run, Pallas kernels for 0% -> 2%
where the time goes in v3:
time: 69.1 us; the launch traced here: 68.8 us
  blocking collectives  58 us (84%)
  starting transfers between devices  5.39 us (8%)
  Pallas kernels  3.84 us (6%)
  local copies, waits for them, and re-layouts  0.72 us (1%)
  between operations  0.72 us (1%)
    all_to_all x1, blocking collectives, shards(): packed = lax.all_to_all(packed, 'feat', 0, 0, tiled=True)  16.1 us
    all_to_all x1, blocking collectives, shards(): grads = lax.all_to_all(grads, ('x', 'z'), 0, 0, tiled=True)  13.4 us
    all_to_all x1, blocking collectives, shards(): lax.all_to_all(grads.reshape(2 * feat_count, 2 * width + 8, rows_own), ('...  12.2 us
    all_gather x1, blocking collectives, shards(): pair = lax.all_gather(feats, 'c')  10.3 us
    all_gather x1, blocking collectives, shards(): pair = lax.all_gather(grads, 'c')  5.98 us
    ppermute x1, starting transfers between devices, shards(): far = lax.ppermute(feats, VERTEX, away)  5.39 us
    pallas_call x1, Pallas kernels, shards(): call(functools.partial(places_kernel, blocks * vertex_count), jax.ShapeDt...  1.43 us
  transfers between devices with their start and end apart: 1, of which 0 were waited for; matrix products, arithmetic and copies ran while one was open for 0% of the time, Pallas kernels for 2%

profile of v3, /device:TPU:1, one launch (start us, length us, event | category | flops | bytes accessed | tf_op | source)
XLA Modules:
  0.0 68.8 jit_solution(4481021661589389307)
XLA Ops:
  0.6 5.4 %collective-permute-start = (bf16[16,1024]{1,0:T(8,128)(2,1)}, bf16[16,1024]{1,0:T(8,128)(2,1)S(1)}, u32[]{:S(2)}, u32[]{:S(2)}) collective-permute-start(bf16[16,1024]{1,0:T(8,128)(2,1)} %bitcast.12), channel_id=1, source_target_pairs={{0,504},{8,16},{16,8},{24,32},{32,24},{40,48},{48,40},{56,64},{64,... | collective-permute-start | bytes 98312 | tf_op jit(solution)/shard_map/ppermute | solution.py:124
  6.0 0.1 pad_add_fusion.place_ref
  6.1 0.0 copy-start.7
  6.1 0.7 copy-done.7
  6.8 0.0 copy-start.1
  6.8 0.0 copy-start
  6.8 0.0 copy-start.3
  6.8 0.0 copy-start.4
  6.8 0.0 copy-start.5
  6.8 1.4 %shard_map.111.spots_ref = s32[8,6]{1,0:T(8,128)S(1)} custom-call(s32[8,6]{1,0:T(8,128)S(1)} %copy-done.7, s32[2]{0:T(128)S(1)} %pad_add_fusion.place_ref), custom_call_target="tpu_custom_call" | custom-call | flops 5000000000 | bytes 2000000 | tf_op jit(solution)/shard_map/pallas_call | solution.py:129
  8.3 0.0 copy-done.1
  8.3 0.0 copy-start.2
  8.3 0.0 copy-start.6
  8.3 10.3 %all-gather = bf16[32,1024]{1,0:T(8,128)(2,1)S(1)} all-gather(bf16[16,1024]{1,0:T(8,128)(2,1)S(1)} %bitcast.13), channel_id=2, replica_groups=mesh['x'=4,'z'=8,'c'=2,'feat'=8] {'c'}, dimensions={0}, use_global_device_ids=true | all-gather | bytes 98304 | tf_op jit(solution)/shard_map/all_gather | solution.py:125
  18.6 0.0 collective-permute-done.far_ref
  18.6 0.0 copy-done
  18.6 0.0 copy-done.3
  18.6 0.0 copy-done.4
  18.7 0.0 copy-done.5
  18.7 1.1 %shard_map.112 = bf16[8,96,128]{2,1,0:T(8,128)(2,1)S(1)} custom-call(s32[8,6]{1,0:T(8,128)S(1)} %shard_map.111.spots_ref, bf16[2,16,1024]{2,1,0:T(8,128)(2,1)S(1)} %bitcast.9, bf16[16,1024]{1,0:T(8,128)(2,1)S(1)} %collective-permute-done.far_ref, bf16[16,1024]{1,0:T(8,128)(2,1)S(1)} %bitcast.14, bf16[8,6,128,128]{3,2,1,0:T(8,128)(2,1)S(1)} %copy-done, ...), custom_call_target="tpu_custom_call" | custom-call | flops 25165824 | bytes 2000000 | tf_op jit(solution)/shard_map/pallas_call | solution.py:136
  19.8 16.1 %all_to_all.15.packed_ref = bf16[8,96,128]{2,1,0:T(8,128)(2,1)S(1)} all-to-all(bf16[8,96,128]{2,1,0:T(8,128)(2,1)S(1)} %shard_map.112), channel_id=1, replica_groups=mesh['x'=4,'z'=8,'c'=2,'feat'=8] {'feat'}, dimensions={0} | all-to-all | bytes 393216 | tf_op jit(solution)/shard_map/all_to_all | solution.py:144
  35.9 0.0 copy-done.2
  35.9 0.0 copy-done.6
  35.9 0.5 shard_map.113
  36.4 12.2 %all_to_all.16.rows_ref = bf16[16,40,128]{2,1,0:T(8,128)(2,1)S(1)} all-to-all(bf16[16,40,128]{2,1,0:T(8,128)(2,1)S(1)} %bitcast.10), channel_id=1, replica_groups=mesh['x'=4,'z'=8,'c'=2,'feat'=8] {'c','feat'}, dimensions={0} | all-to-all | bytes 327680 | tf_op jit(solution)/shard_map/all_to_all | solution.py:155
  48.7 13.4 %all_to_all.17.rows_ref = bf16[32,40,128]{2,1,0:T(8,128)(2,1)S(1)} all-to-all(bf16[32,40,128]{2,1,0:T(8,128)(2,1)S(1)} %shard_map.114), channel_id=1, replica_groups=mesh['x'=4,'z'=8,'c'=2,'feat'=8] {'x','z'}, dimensions={0} | all-to-all | bytes 655360 | tf_op jit(solution)/shard_map/all_to_all | solution.py:161
  62.1 0.1 shard_map.115
  62.2 6.0 %all-gather.1 = f32[80,128]{1,0:T(8,128)S(1)} all-gather(f32[40,128]{1,0:T(8,128)S(1)} %shard_map.115), channel_id=3, replica_groups=mesh['x'=4,'z'=8,'c'=2,'feat'=8] {'c'}, dimensions={0}, use_global_device_ids=true | all-gather | bytes 61440 | tf_op jit(solution)/shard_map/all_gather | solution.py:163
  68.1 0.6 shard_map.116
  (1 shorter events, 0.0 us)
Async XLA Ops:
  0.6 18.0 %collective-permute-start = (bf16[16,1024]{1,0:T(8,128)(2,1)}, bf16[16,1024]{1,0:T(8,128)(2,1)S(1)}, u32[]{:S(2)}, u32[]{:S(2)}) collective-permute-start(bf16[16,1024]{1,0:T(8,128)(2,1)} %bitcast.12), channel_id=1, source_target_pairs={{0,504},{8,16},{16,8},{24,32},{32,24},{40,48},{48,40},{56,64},{64,... | collective-permute-start | bytes 98312 | tf_op jit(solution)/shard_map/ppermute | solution.py:124
  6.1 0.7 copy-start.7
  6.8 1.5 %copy-start.1 = (bf16[1024,16]{0,1:T(8,128)(2,1)S(1)}, bf16[1024,16]{0,1:T(8,128)(2,1)}, u32[]{:S(2)}) copy-start(bf16[1024,16]{0,1:T(8,128)(2,1)} %param.8) | copy-start | bytes 98308
  6.8 11.8 %copy-start = (bf16[8,6,128,128]{3,2,1,0:T(8,128)(2,1)S(1)}, bf16[8,6,128,128]{3,2,1,0:T(8,128)(2,1)}, u32[]{:S(2)}) copy-start(bf16[8,6,128,128]{3,2,1,0:T(8,128)(2,1)} %adj_ref.1) | copy-start | bytes 4718596
  6.8 11.8 %copy-start.3 = (bf16[16,256]{1,0:T(8,128)(2,1)S(1)}, bf16[16,256]{1,0:T(8,128)(2,1)}, u32[]{:S(2)}) copy-start(bf16[16,256]{1,0:T(8,128)(2,1)} %ws_ref.1) | copy-start | bytes 24580
  6.8 11.8 %copy-start.4 = (bf16[16,256]{1,0:T(8,128)(2,1)S(1)}, bf16[16,256]{1,0:T(8,128)(2,1)}, u32[]{:S(2)}) copy-start(bf16[16,256]{1,0:T(8,128)(2,1)} %wn_ref.1) | copy-start | bytes 24580
  6.8 11.8 %copy-start.5 = (s32[1024]{0:T(1024)S(1)}, s32[1024]{0:T(1024)}, u32[]{:S(2)}) copy-start(s32[1024]{0:T(1024)} %param.11) | copy-start | bytes 12292
  8.3 27.6 %copy-start.2 = (bf16[128,256]{1,0:T(8,128)(2,1)S(1)}, bf16[128,256]{1,0:T(8,128)(2,1)}, u32[]{:S(2)}) copy-start(bf16[128,256]{1,0:T(8,128)(2,1)} %cot_ref.1) | copy-start | bytes 196612
  8.3 27.6 %copy-start.6 = (f32[256]{0:T(256)S(1)}, f32[256]{0:T(256)}, u32[]{:S(2)}) copy-start(f32[256]{0:T(256)} %param.14) | copy-start | bytes 3076

commit v4 on v3

--- a/solution.py
+++ b/solution.py
@@ -9,7 +9,8 @@
 
 F32 = jnp.float32
 BF16 = jnp.bfloat16
-VERTEX = ("x", "z", "c")
+CHIPS = ("x", "z", "near")
+VERTEX = ("x", "z", "near", "c")
 NT = (((1,), (1,)), ((), ()))
 TN = (((0,), (0,)), ((), ()))
 VMEM = pl.BlockSpec(memory_space=pltpu.VMEM)
@@ -68,10 +69,12 @@
     feat_count = packed_ref.shape[0]
     rows = packed_ref.shape[2]
     half = rows
+    pairs = width // 4
     inputs = packed_ref[:, : 2 * width].reshape(feat_count * 2 * width, rows)
     left = packed_ref[:, 2 * width : 4 * width].reshape(feat_count * 2 * width, half)
     right = packed_ref[:, 4 * width : 6 * width].reshape(feat_count * 2 * width, half)
     ones = jnp.ones((8, rows), BF16)
+    bias = []
     for h, weights in enumerate((left, right)):
         lanes = slice(h * half, (h + 1) * half)
         preact = lax.dot_general(inputs, weights, TN, preferred_element_type=F32) + bias_ref[:, lanes]
@@ -79,35 +82,51 @@
         cot = cot_ref[:, lanes].astype(F32)
         grad_pre = jnp.where(preact > 0, cot, 0.0).astype(BF16)
         grads = jnp.dot(inputs, grad_pre, preferred_element_type=F32)
-        grads = grads.reshape(feat_count, 2, width, half)
-        bias = jnp.dot(ones, grad_pre, preferred_element_type=F32).astype(grads_ref.dtype)
+        bias.append(jnp.dot(ones, grad_pre, preferred_element_type=F32)[:1])
+        for f in range(feat_count):
+            for c in range(2):
+                for near in range(2):
+                    first = (f * 2 + c) * width + near * 2 * pairs
+                    for i in range(pairs):
+                        pair = grads[first + 2 * i : first + 2 * i + 2]
+                        grads_ref[near, c, f, h * pairs + i] = pair.astype(BF16)
+    bias = jnp.concatenate(bias, axis=0).astype(BF16)
+    for f in range(feat_count):
         for c in range(2):
-            for f in range(feat_count):
-                grads_ref[c, f, h * width : (h + 1) * width] = grads[f, c].astype(grads_ref.dtype)
-                if c == h:
-                    grads_ref[c, f, 2 * width :] = bias
+            for near in range(2):
+                grads_ref[near, c, f, 2 * pairs] = bias
 
 
 def sum_kernel(rows_ref, out_ref):
     total = rows_ref[0].astype(F32)
     for i in range(1, rows_ref.shape[0]):
         total += rows_ref[i].astype(F32)
-    if len(out_ref.shape) == 2:
-        out_ref[...] = total.astype(out_ref.dtype)
-    else:
-        total = total.astype(out_ref.dtype)
-        for i in range(out_ref.shape[0]):
-            out_ref[i] = total
-
-
-def unpack_kernel(width, pair_ref, layer_ref, hidden_ref, self_ref, neigh_ref, bias_ref):
+    total = total.astype(out_ref.dtype)
+    for i in range(out_ref.shape[0]):
+        out_ref[i] = total
+
+
+def total_kernel(rows_ref, grads_ref, bias_ref):
+    pairs = (rows_ref.shape[1] - 1) // 2
+    half = rows_ref.shape[3]
+    for near in range(2):
+        total = rows_ref[near].astype(F32)
+        for i in range(near + 2, rows_ref.shape[0], 2):
+            total += rows_ref[i].astype(F32)
+        for h in range(2):
+            lanes = slice(h * half, (h + 1) * half)
+            for i in range(pairs):
+                first = 2 * (near * pairs + i)
+                grads_ref[first : first + 2, lanes] = total[h * pairs + i]
+            if near == 0:
+                bias_ref[:, lanes] = total[2 * pairs, h : h + 1]
+
+
+def output_kernel(pair_ref, total_ref, layer_ref, hidden_ref, self_ref, neigh_ref, bias_ref):
     hidden_ref[...] = layer_ref[...]
-    half = pair_ref.shape[2]
-    for h in range(2):
-        lanes = slice(h * half, (h + 1) * half)
-        self_ref[:, lanes] = pair_ref[0, h * width : (h + 1) * width]
-        neigh_ref[:, lanes] = pair_ref[1, h * width : (h + 1) * width]
-        bias_ref[:, lanes] = pair_ref[h, 2 * width : 2 * width + 1]
+    self_ref[...] = pair_ref[0]
+    neigh_ref[...] = pair_ref[1]
+    bias_ref[...] = total_ref[...]
 
 
 def shards(node_feats, adj_tiles, tile_cols, degrees, w_self, w_neigh, hidden_bias, cotangent):
@@ -142,40 +161,46 @@
     )(spots, pair, far, feats, adj_tiles, degrees.reshape(1, -1), w_self, w_neigh)
 
     packed = lax.all_to_all(packed, "feat", 0, 0, tiled=True)
+    near_count = lax.axis_size("near")
+    peers = near_count * 2 * feat_count
+    pieces = (width // 2 + 1, 2, rows_own)
     hidden, grads = call(
         functools.partial(layer_kernel, width),
         (
             jax.ShapeDtypeStruct((rows_own, hidden_units), BF16),
-            jax.ShapeDtypeStruct((2, feat_count, 2 * width + 8, rows_own), BF16),
+            jax.ShapeDtypeStruct((near_count, 2, feat_count, *pieces), BF16),
         ),
         [VMEM] * 3,
         flops=4 * rows_own * 256 * hidden_units,
     )(packed, cotangent, hidden_bias.reshape(1, -1))
 
-    grads = lax.all_to_all(
-        grads.reshape(2 * feat_count, 2 * width + 8, rows_own), ("c", "feat"), 0, 0, tiled=True
-    )
-    grads = call(
-        sum_kernel, jax.ShapeDtypeStruct((chip_count, 2 * width + 8, rows_own), BF16), [VMEM]
+    grads = lax.all_to_all(grads.reshape(peers, *pieces), ("near", "c", "feat"), 0, 0, tiled=True)
+    grads = call(sum_kernel, jax.ShapeDtypeStruct((chip_count, *pieces), BF16), [VMEM])(grads)
+    grads = lax.all_to_all(grads, CHIPS, 0, 0, tiled=True)
+    grads, grad_bias = call(
+        total_kernel,
+        (
+            jax.ShapeDtypeStruct((width, hidden_units), F32),
+            jax.ShapeDtypeStruct((1, hidden_units), F32),
+        ),
+        [VMEM],
     )(grads)
-    grads = lax.all_to_all(grads, ("x", "z"), 0, 0, tiled=True)
-    grads = call(sum_kernel, jax.ShapeDtypeStruct((2 * width + 8, rows_own), F32), [VMEM])(grads)
     pair = lax.all_gather(grads, "c")
     hidden, grad_self, grad_neigh, grad_bias = call(
-        functools.partial(unpack_kernel, width),
+        output_kernel,
         (
             jax.ShapeDtypeStruct((rows_own, hidden_units), BF16),
             jax.ShapeDtypeStruct((width, hidden_units), F32),
             jax.ShapeDtypeStruct((width, hidden_units), F32),
             jax.ShapeDtypeStruct((1, hidden_units), F32),
         ),
-        [VMEM] * 2,
-    )(pair, hidden)
+        [VMEM] * 3,
+    )(pair, grad_bias, hidden)
     return (hidden, grad_self, grad_neigh, grad_bias.reshape(hidden_units))
 
 
 def solution(mesh):
-    sizes = {"x": 4, "z": 8, "c": 2, "feat": 8}
+    sizes = {"x": 4, "z": 4, "near": 2, "c": 2, "feat": 8}
     grid = Mesh(mesh.devices.reshape(tuple(sizes.values())), tuple(sizes))
     return jax.shard_map(
         shards,

time: 69.1 us -> 68.7 us (level)
    all_gather x1, blocking collectives: 5.98 us -> 3.77 us  [shards(): pair = lax.all_gather(grads, 'c')]
    all_to_all x2, blocking collectives: 25.6 us -> 27.3 us  [the longest x1 14.7 us: shards(): lax.all_to_all(grads.reshape(peers, *pieces), ('near', 'c', 'feat'), 0, 0...]
where the time goes in v4:
time: 68.7 us; the launch traced here: 68.4 us
  blocking collectives  57.5 us (84%)
  starting transfers between devices  5.39 us (8%)
  Pallas kernels  3.95 us (6%)
  between operations  0.73 us (1%)
  local copies, waits for them, and re-layouts  0.72 us (1%)
    all_to_all x1, blocking collectives, shards(): packed = lax.all_to_all(packed, 'feat', 0, 0, tiled=True)  16.1 us
    all_to_all x1, blocking collectives, shards(): lax.all_to_all(grads.reshape(peers, *pieces), ('near', 'c', 'feat'), 0, 0...  14.7 us
    all_to_all x1, blocking collectives, shards(): grads = lax.all_to_all(grads, CHIPS, 0, 0, tiled=True)  12.6 us
    all_gather x1, blocking collectives, shards(): pair = lax.all_gather(feats, 'c')  10.3 us
    ppermute x1, starting transfers between devices, shards(): far = lax.ppermute(feats, VERTEX, away)  5.39 us
    all_gather x1, blocking collectives, shards(): pair = lax.all_gather(grads, 'c')  3.77 us
    pallas_call x1, Pallas kernels, shards(): call(functools.partial(places_kernel, blocks * vertex_count), jax.ShapeDt...  1.43 us
  transfers between devices with their start and end apart: 1, of which 0 were waited for; matrix products, arithmetic and copies ran while one was open for 0% of the time, Pallas kernels for 2%

profile of v4, /device:TPU:1, one launch (start us, length us, event | category | flops | bytes accessed | tf_op | source)
XLA Modules:
  0.0 68.4 jit_solution(3326630955685962964)
XLA Ops:
  0.6 5.4 %collective-permute-start = (bf16[16,1024]{1,0:T(8,128)(2,1)}, bf16[16,1024]{1,0:T(8,128)(2,1)S(1)}, u32[]{:S(2)}, u32[]{:S(2)}) collective-permute-start(bf16[16,1024]{1,0:T(8,128)(2,1)} %bitcast.11), channel_id=1, source_target_pairs={{0,504},{8,16},{16,8},{24,32},{32,24},{40,48},{48,40},{56,64},{64,... | collective-permute-start | bytes 98312 | tf_op jit(solution)/shard_map/ppermute | solution.py:143
  6.0 0.1 pad_add_fusion.place_ref
  6.1 0.0 copy-start.7
  6.1 0.7 %copy-done.7 = s32[8,6]{1,0:T(8,128)S(1)} copy-done((s32[8,6]{1,0:T(8,128)S(1)}, s32[8,6]{1,0:T(8,128)}, u32[]{:S(2)}) %copy-start.7) | copy-done | bytes 216
  6.8 0.0 copy-start.1
  6.8 0.0 copy-start
  6.8 0.0 copy-start.3
  6.8 0.0 copy-start.4
  6.8 0.0 copy-start.5
  6.8 1.4 %shard_map.111.spots_ref = s32[8,6]{1,0:T(8,128)S(1)} custom-call(s32[8,6]{1,0:T(8,128)S(1)} %copy-done.7, s32[2]{0:T(128)S(1)} %pad_add_fusion.place_ref), custom_call_target="tpu_custom_call" | custom-call | flops 5000000000 | bytes 2000000 | tf_op jit(solution)/shard_map/pallas_call | solution.py:148
  8.3 0.0 copy-done.1
  8.3 0.0 copy-start.2
  8.3 0.0 copy-start.6
  8.3 10.3 %all-gather = bf16[32,1024]{1,0:T(8,128)(2,1)S(1)} all-gather(bf16[16,1024]{1,0:T(8,128)(2,1)S(1)} %bitcast.12), channel_id=2, replica_groups=mesh['x'=4,'z'=4,'near'=2,'c'=2,'feat'=8] {'c'}, dimensions={0}, use_global_device_ids=true | all-gather | bytes 98304 | tf_op jit(solution)/shard_map/all_gather | solution.py:144
  18.6 0.0 collective-permute-done.far_ref
  18.6 0.0 copy-done
  18.6 0.0 copy-done.3
  18.6 0.0 copy-done.4
  18.7 0.0 copy-done.5
  18.7 1.1 %shard_map.112 = bf16[8,96,128]{2,1,0:T(8,128)(2,1)S(1)} custom-call(s32[8,6]{1,0:T(8,128)S(1)} %shard_map.111.spots_ref, bf16[2,16,1024]{2,1,0:T(8,128)(2,1)S(1)} %bitcast.9, bf16[16,1024]{1,0:T(8,128)(2,1)S(1)} %collective-permute-done.far_ref, bf16[16,1024]{1,0:T(8,128)(2,1)S(1)} %bitcast.13, bf16[8,6,128,128]{3,2,1,0:T(8,128)(2,1)S(1)} %copy-done, ...), custom_call_target="tpu_custom_call" | custom-call | flops 25165824 | bytes 2000000 | tf_op jit(solution)/shard_map/pallas_call | solution.py:155
  19.8 16.1 %all_to_all.15.packed_ref = bf16[8,96,128]{2,1,0:T(8,128)(2,1)S(1)} all-to-all(bf16[8,96,128]{2,1,0:T(8,128)(2,1)S(1)} %shard_map.112), channel_id=1, replica_groups=mesh['x'=4,'z'=4,'near'=2,'c'=2,'feat'=8] {'feat'}, dimensions={0} | all-to-all | bytes 393216 | tf_op jit(solution)/shard_map/all_to_all | solution.py:163
  35.9 0.0 copy-done.2
  35.9 0.0 copy-done.6
  35.9 0.6 shard_map.113
  36.4 14.7 %all_to_all.16.rows_ref = bf16[32,9,2,128]{3,2,1,0:T(2,128)(2,1)S(1)} all-to-all(bf16[32,9,2,128]{3,2,1,0:T(2,128)(2,1)S(1)} %bitcast.10), channel_id=1, replica_groups=mesh['x'=4,'z'=4,'near'=2,'c'=2,'feat'=8] {'near','c','feat'}, dimensions={0} | all-to-all | bytes 294912 | tf_op jit(solution)/shard_map/all_to_all | solution.py:177
  51.1 0.1 shard_map.114
  51.2 12.6 %all_to_all.17.rows_ref = bf16[32,9,2,128]{3,2,1,0:T(2,128)(2,1)S(1)} all-to-all(bf16[32,9,2,128]{3,2,1,0:T(2,128)(2,1)S(1)} %shard_map.114), channel_id=1, replica_groups=mesh['x'=4,'z'=4,'near'=2,'c'=2,'feat'=8] {'x','z','near'}, dimensions={0} | all-to-all | bytes 294912 | tf_op jit(solution)/shard_map/all_to_all | solution.py:179
  63.9 0.1 shard_map.115
  64.0 3.8 %all-gather.1 = f32[32,256]{1,0:T(8,128)S(1)} all-gather(f32[16,256]{1,0:T(8,128)S(1)} %get-tuple-element.13), channel_id=3, replica_groups=mesh['x'=4,'z'=4,'near'=2,'c'=2,'feat'=8] {'c'}, dimensions={0}, use_global_device_ids=true | all-gather | bytes 49152 | tf_op jit(solution)/shard_map/all_gather | solution.py:188
  67.7 0.6 shard_map.116
Async XLA Ops:
  0.6 18.0 %collective-permute-start = (bf16[16,1024]{1,0:T(8,128)(2,1)}, bf16[16,1024]{1,0:T(8,128)(2,1)S(1)}, u32[]{:S(2)}, u32[]{:S(2)}) collective-permute-start(bf16[16,1024]{1,0:T(8,128)(2,1)} %bitcast.11), channel_id=1, source_target_pairs={{0,504},{8,16},{16,8},{24,32},{32,24},{40,48},{48,40},{56,64},{64,... | collective-permute-start | bytes 98312 | tf_op jit(solution)/shard_map/ppermute | solution.py:143
  6.1 0.7 %copy-start.7 = (s32[8,6]{1,0:T(8,128)S(1)}, s32[8,6]{1,0:T(8,128)}, u32[]{:S(2)}) copy-start(s32[8,6]{1,0:T(8,128)} %cols_ref.1) | copy-start | bytes 580
  6.8 1.5 %copy-start.1 = (bf16[1024,16]{0,1:T(8,128)(2,1)S(1)}, bf16[1024,16]{0,1:T(8,128)(2,1)}, u32[]{:S(2)}) copy-start(bf16[1024,16]{0,1:T(8,128)(2,1)} %param.8) | copy-start | bytes 98308
  6.8 11.8 %copy-start = (bf16[8,6,128,128]{3,2,1,0:T(8,128)(2,1)S(1)}, bf16[8,6,128,128]{3,2,1,0:T(8,128)(2,1)}, u32[]{:S(2)}) copy-start(bf16[8,6,128,128]{3,2,1,0:T(8,128)(2,1)} %adj_ref.1) | copy-start | bytes 4718596
  6.8 11.8 %copy-start.3 = (bf16[16,256]{1,0:T(8,128)(2,1)S(1)}, bf16[16,256]{1,0:T(8,128)(2,1)}, u32[]{:S(2)}) copy-start(bf16[16,256]{1,0:T(8,128)(2,1)} %ws_ref.1) | copy-start | bytes 24580
  6.8 11.8 %copy-start.4 = (bf16[16,256]{1,0:T(8,128)(2,1)S(1)}, bf16[16,256]{1,0:T(8,128)(2,1)}, u32[]{:S(2)}) copy-start(bf16[16,256]{1,0:T(8,128)(2,1)} %wn_ref.1) | copy-start | bytes 24580
  6.8 11.8 %copy-start.5 = (s32[1024]{0:T(1024)S(1)}, s32[1024]{0:T(1024)}, u32[]{:S(2)}) copy-start(s32[1024]{0:T(1024)} %param.11) | copy-start | bytes 12292
  8.3 27.6 %copy-start.2 = (bf16[128,256]{1,0:T(8,128)(2,1)S(1)}, bf16[128,256]{1,0:T(8,128)(2,1)}, u32[]{:S(2)}) copy-start(bf16[128,256]{1,0:T(8,128)(2,1)} %cot_ref.1) | copy-start | bytes 196612
  8.3 27.6 %copy-start.6 = (f32[256]{0:T(256)S(1)}, f32[256]{0:T(256)}, u32[]{:S(2)}) copy-start(f32[256]{0:T(256)} %param.14) | copy-start | bytes 3076

commit v5 on v3

v5 whole, which is shorter than its diff:
```python
import functools

import jax
import jax.numpy as jnp
from jax import lax
from jax.experimental import pallas as pl
from jax.experimental.pallas import tpu as pltpu
from jax.sharding import Mesh, PartitionSpec as P

F32 = jnp.float32
BF16 = jnp.bfloat16
CHIPS = ("x", "z", "near")
VERTEX = ("x", "z", "near", "c")
NT = (((1,), (1,)), ((), ()))
TN = (((0,), (0,)), ((), ()))
VMEM = pl.BlockSpec(memory_space=pltpu.VMEM)
SMEM = pl.BlockSpec(memory_space=pltpu.SMEM)


def call(kernel, out_shape, in_specs, scratch_shapes=(), flops=0, out_specs=None):
    if out_specs is None:
        out_specs = [VMEM] * len(out_shape) if isinstance(out_shape, tuple) else VMEM
    return pl.pallas_call(
        kernel,
        out_shape=out_shape,
        in_specs=in_specs,
        out_specs=out_specs,
        scratch_shapes=list(scratch_shapes),
        compiler_params=pltpu.CompilerParams(vmem_limit_bytes=32 * 1024 * 1024),
        cost_estimate=pl.CostEstimate(flops=flops, bytes_accessed=2000000, transcendentals=0),
    )


def place_kernel(blocks, where_ref, place_ref):
    place_ref[...] = where_ref[...] * blocks


def aggregate_kernel(total_blocks, cols_ref, place_ref, pair_ref, far_ref, adj_ref, deg_ref, ws_ref, wn_ref, out_ref, feats):
    blocks, tiles, _, size = adj_ref.shape
    width = far_ref.shape[0]
    half = ws_ref.shape[1] // 2
    for b in range(blocks):
        feats[b] = pair_ref[0, :, b * size : (b + 1) * size]
        feats[blocks + b] = pair_ref[1, :, b * size : (b + 1) * size]
        feats[2 * blocks + b] = far_ref[:, b * size : (b + 1) * size]
    first = place_ref[0, 0]
    turn = place_ref[1, 0]
    own = place_ref[2, 0]

    def spot(col):
        col = col - first + blocks
        col = jnp.where(col < 0, col + total_blocks, col)
        col = jnp.where(col >= total_blocks, col - total_blocks, col) + turn
        return jnp.where(col >= 3 * blocks, col - 3 * blocks, col)

    for r in range(blocks):
        picked = jnp.concatenate([feats[spot(cols_ref[r, k])] for k in range(tiles)], axis=1)
        weights = jnp.concatenate([adj_ref[r, k] for k in range(tiles)], axis=1)
        total = lax.dot_general(picked, weights, NT, preferred_element_type=F32)
        degree = deg_ref[:, r * size : (r + 1) * size].astype(F32)
        out_ref[r, :width] = feats[own + r]
        out_ref[r, width : 2 * width] = (total / degree).astype(BF16)
        for h in range(2):
            at = 2 * width * (1 + h)
            out_ref[r, at : at + width] = ws_ref[:, h * half : (h + 1) * half]
            out_ref[r, at + width : at + 2 * width] = wn_ref[:, h * half : (h + 1) * half]


def forward_kernel(width, packed_ref, cot_ref, bias_ref, hidden_ref, share_ref):
    feat_count = packed_ref.shape[0]
    rows = packed_ref.shape[2]
    depth = feat_count * 2 * width
    half = rows
    inputs = packed_ref[:, : 2 * width].reshape(depth, rows)
    left = packed_ref[:, 2 * width : 4 * width].reshape(depth, half)
    right = packed_ref[:, 4 * width : 6 * width].reshape(depth, half)
    share_ref[:depth] = inputs
    for h, weights in enumerate((left, right)):
        lanes = slice(h * half, (h + 1) * half)
        preact = lax.dot_general(inputs, weights, TN, preferred_element_type=F32) + bias_ref[:, lanes]
        hidden_ref[:, lanes] = jnp.maximum(preact, 0.0).astype(BF16)
        cot = cot_ref[:, lanes].astype(F32)
        share_ref[depth + h * rows : depth + (h + 1) * rows] = jnp.where(preact > 0, cot, 0.0).astype(BF16)


def backward_kernel(width, pair_ref, place_ref, grads_ref):
    feat_count = grads_ref.shape[1]
    pairs = width // 2
    depth = feat_count * 2 * width
    rows = (pair_ref.shape[1] - depth) // 2
    core = jnp.broadcast_to(place_ref[2:3], (rows, pair_ref.shape[2]))
    inputs = jnp.concatenate([pair_ref[c, :depth] for c in range(2)], axis=1)
    grad_pre = jnp.concatenate(
        [
            jnp.where(
                core == 0,
                pair_ref[c, depth : depth + rows].astype(F32),
                pair_ref[c, depth + rows :].astype(F32),
            ).astype(BF16)
            for c in range(2)
        ],
        axis=0,
    )
    grads = jnp.dot(inputs, grad_pre, preferred_element_type=F32)
    ones = jnp.ones((8, 2 * rows), BF16)
    bias = jnp.dot(ones, grad_pre, preferred_element_type=F32)[:1]
    bias = jnp.concatenate([bias, jnp.zeros_like(bias)], axis=0).astype(BF16)
    for f in range(feat_count):
        for near in range(2):
            for i in range(pairs):
                first = (f * 2 + near) * width + 2 * i
                grads_ref[near, f, i] = grads[first : first + 2].astype(BF16)
            grads_ref[near, f, pairs] = bias


def sum_kernel(rows_ref, out_ref):
    total = rows_ref[0].astype(F32)
    for i in range(1, rows_ref.shape[0]):
        total += rows_ref[i].astype(F32)
    total = total.astype(out_ref.dtype)
    for i in range(out_ref.shape[0]):
        out_ref[i] = total


def total_kernel(rows_ref, out_ref):
    pairs = rows_ref.shape[1] - 1
    for near in range(2):
        total = rows_ref[near].astype(F32)
        for i in range(near + 2, rows_ref.shape[0], 2):
            total += rows_ref[i].astype(F32)
        for i in range(pairs):
            first = 2 * (near * pairs + i)
            out_ref[first : first + 2] = total[i]
        if near == 0:
            out_ref[4 * pairs :] = jnp.zeros((out_ref.shape[0] - 4 * pairs, out_ref.shape[1]), F32)
            out_ref[4 * pairs : 4 * pairs + 2] = total[pairs]


def output_kernel(pair_ref, layer_ref, hidden_ref, self_ref, neigh_ref, bias_ref):
    width = self_ref.shape[0]
    half = pair_ref.shape[2]
    hidden_ref[...] = layer_ref[...]
    for h in range(2):
        lanes = slice(h * half, (h + 1) * half)
        self_ref[:, lanes] = pair_ref[h, :width]
        neigh_ref[:, lanes] = pair_ref[h, width : 2 * width]
        bias_ref[:, lanes] = pair_ref[h, 2 * width : 2 * width + 1]


def shards(node_feats, adj_tiles, tile_cols, degrees, w_self, w_neigh, hidden_bias, cotangent):
    node_count, width = node_feats.shape
    blocks, tiles, size, _ = adj_tiles.shape
    vertex_count = lax.axis_size(VERTEX)
    feat_count = lax.axis_size("feat")
    chip_count = vertex_count // 2
    rows_own = node_count // feat_count
    hidden_units = w_self.shape[1]

    feats = node_feats.T
    away = [(v, (v - 1 if v % 2 == 0 else v + 1) % vertex_count) for v in range(vertex_count)]
    far = lax.ppermute(feats, VERTEX, away)
    pair = lax.all_gather(feats, "c")
    vertex_idx = lax.axis_index(VERTEX)
    core = lax.axis_index("c")
    where = jnp.stack([vertex_idx, 2 * (1 - core), core]).astype(jnp.int32)
    place = call(
        functools.partial(place_kernel, blocks),
        jax.ShapeDtypeStruct((3, size), jnp.int32),
        [VMEM],
        flops=5 * 10**9,
    )(jnp.broadcast_to(where[:, None], (3, size)))
    packed = call(
        functools.partial(aggregate_kernel, blocks * vertex_count),
        jax.ShapeDtypeStruct((feat_count, 6 * width, rows_own), BF16),
        [SMEM] * 2 + [VMEM] * 6,
        [pltpu.VMEM((3 * blocks, width, size), BF16)],
        flops=2 * blocks * tiles * size * size * width,
    )(tile_cols, place, pair, far, adj_tiles, degrees.reshape(1, -1), w_self, w_neigh)

    packed = lax.all_to_all(packed, "feat", 0, 0, tiled=True)
    near_count = lax.axis_size("near")
    depth = feat_count * 2 * width
    pieces = (width // 2 + 1, 2, rows_own)
    hidden, share = call(
        functools.partial(forward_kernel, width),
        (
            jax.ShapeDtypeStruct((rows_own, hidden_units), BF16),
            jax.ShapeDtypeStruct((depth + 2 * rows_own, rows_own), BF16),
        ),
        [VMEM] * 3,
        flops=2 * rows_own * depth * hidden_units,
    )(packed, cotangent, hidden_bias.reshape(1, -1))
    pair = lax.all_gather(share, "c")
    grads = call(
        functools.partial(backward_kernel, width),
        jax.ShapeDtypeStruct((near_count, feat_count, *pieces), BF16),
        [VMEM] * 2,
        flops=2 * rows_own * depth * hidden_units,
    )(pair, place)

    grads = lax.all_to_all(grads.reshape(near_count * feat_count, *pieces), ("near", "feat"), 0, 0, tiled=True)
    grads = call(sum_kernel, jax.ShapeDtypeStruct((chip_count, *pieces), BF16), [VMEM])(grads)
    grads = lax.all_to_all(grads, CHIPS, 0, 0, tiled=True)
    grads = call(total_kernel, jax.ShapeDtypeStruct((2 * width + 8, rows_own), F32), [VMEM])(grads)
    pair = lax.all_gather(grads, "c")
    hidden, grad_self, grad_neigh, grad_bias = call(
        output_kernel,
        (
            jax.ShapeDtypeStruct((rows_own, hidden_units), BF16),
            jax.ShapeDtypeStruct((width, hidden_units), F32),
            jax.ShapeDtypeStruct((width, hidden_units), F32),
            jax.ShapeDtypeStruct((1, hidden_units), F32),
        ),
        [VMEM] * 2,
    )(pair, hidden)
    return (hidden, grad_self, grad_neigh, grad_bias.reshape(hidden_units))


def solution(mesh):
    sizes = {"x": 4, "z": 4, "near": 2, "c": 2, "feat": 8}
    grid = Mesh(mesh.devices.reshape(tuple(sizes.values())), tuple(sizes))
    return jax.shard_map(
        shards,
        mesh=grid,
        in_specs=(
            P(VERTEX, "feat"),
            P(VERTEX, None, None, None),
            P(VERTEX, None),
            P(VERTEX),
            P("feat", None),
            P("feat", None),
            P(),
            P((*VERTEX, "feat"), None),
        ),
        out_specs=(P((*VERTEX, "feat"), None), P("feat", None), P("feat", None), P()),
        check_vma=False,
    )
```

time: 69.1 us -> 67 us (0.970)
  Pallas kernels: 3.84 us -> 2.38 us
  blocking collectives: 58 us -> 57.3 us
    all_gather x0 -> x1, blocking collectives: none -> 3.61 us  [shards(): pair = lax.all_gather(share, 'c')]
    all_to_all x2, blocking collectives: 25.6 us -> 22.6 us  [the longest x1 12.5 us: shards(): grads = lax.all_to_all(grads, CHIPS, 0, 0, tiled=True)]
    pallas_call x6 -> x7, Pallas kernels: 3.84 us -> 2.38 us  [the longest x1 1.14 us: shards(): call(functools.partial(aggregate_kernel, blocks * vertex_count), jax.Shap...]
    all_gather x1, blocking collectives: 5.98 us -> 4.74 us  [shards(): pair = lax.all_gather(grads, 'c')]
  transfers between devices with their start and end apart: 1 -> 1, of which waited for: 0 -> 0; matrix products, arithmetic and copies ran while one was open for 0% -> 0% of each run, Pallas kernels for 2% -> 0%
where the time goes in v5:
time: 67 us; the launch traced here: 66.7 us
  blocking collectives  57.3 us (86%)
  starting transfers between devices  5.39 us (8%)
  Pallas kernels  2.38 us (4%)
  local copies, waits for them, and re-layouts  0.82 us (1%)
  between operations  0.72 us (1%)
    all_to_all x1, blocking collectives, shards(): packed = lax.all_to_all(packed, 'feat', 0, 0, tiled=True)  16.1 us
    all_to_all x1, blocking collectives, shards(): grads = lax.all_to_all(grads, CHIPS, 0, 0, tiled=True)  12.5 us
    all_gather x1, blocking collectives, shards(): pair = lax.all_gather(feats, 'c')  10.3 us
    all_to_all x1, blocking collectives, shards(): lax.all_to_all(grads.reshape(near_count * feat_count, *pieces), ('near',...  10.1 us
    ppermute x1, starting transfers between devices, shards(): far = lax.ppermute(feats, VERTEX, away)  5.39 us
    all_gather x1, blocking collectives, shards(): pair = lax.all_gather(grads, 'c')  4.74 us
    all_gather x1, blocking collectives, shards(): pair = lax.all_gather(share, 'c')  3.61 us
  transfers between devices with their start and end apart: 1, of which 0 were waited for; matrix products, arithmetic and copies ran while one was open for 0% of the time, Pallas kernels for 0%

profile of v5, /device:TPU:1, one launch (start us, length us, event | category | flops | bytes accessed | tf_op | source)
XLA Modules:
  0.0 66.7 jit_solution(15883331213045635367)
XLA Ops:
  0.6 5.4 %collective-permute-start = (bf16[16,1024]{1,0:T(8,128)(2,1)}, bf16[16,1024]{1,0:T(8,128)(2,1)S(1)}, u32[]{:S(2)}, u32[]{:S(2)}) collective-permute-start(bf16[16,1024]{1,0:T(8,128)(2,1)} %bitcast.17), channel_id=1, source_target_pairs={{0,504},{8,16},{16,8},{24,32},{32,24},{40,48},{48,40},{56,64},{64,... | collective-permute-start | bytes 98312 | tf_op jit(solution)/shard_map/ppermute | solution.py:161
  6.0 0.1 pad_add_fusion
  6.1 0.1 broadcast_in_dim.2.where_ref
  6.2 0.0 copy-start.7
  6.2 0.0 copy-start
  6.2 0.0 copy-start.2
  6.2 0.0 copy-start.3
  6.2 0.0 copy-start.4
  6.2 0.0 copy-start.5
  6.2 0.7 %copy-done.7 = bf16[1024,16]{0,1:T(8,128)(2,1)S(1)} copy-done((bf16[1024,16]{0,1:T(8,128)(2,1)S(1)}, bf16[1024,16]{0,1:T(8,128)(2,1)}, u32[]{:S(2)}) %copy-start.7) | copy-done | bytes 32792
  7.0 0.0 copy-start.1
  7.0 0.0 copy-start.6
  7.0 10.3 %all-gather = bf16[32,1024]{1,0:T(8,128)(2,1)S(1)} all-gather(bf16[16,1024]{1,0:T(8,128)(2,1)S(1)} %bitcast.18), channel_id=2, replica_groups=mesh['x'=4,'z'=4,'near'=2,'c'=2,'feat'=8] {'c'}, dimensions={0}, use_global_device_ids=true | all-gather | bytes 98304 | tf_op jit(solution)/shard_map/all_gather | solution.py:162
  17.3 0.0 collective-permute-done.far_ref
  17.3 0.0 copy-done
  17.3 0.0 copy-done.2
  17.3 0.0 copy-done.3
  17.3 0.0 copy-done.4
  17.3 0.0 copy-done.5
  17.3 1.1 %shard_map.112 = bf16[8,96,128]{2,1,0:T(8,128)(2,1)S(1)} custom-call(s32[8,6]{1,0:T(8,128)S(1)} %copy-done.4, s32[3,128]{1,0:T(4,128)S(1)} %shard_map.111.place_ref, bf16[2,16,1024]{2,1,0:T(8,128)(2,1)S(1)} %bitcast.13, bf16[16,1024]{1,0:T(8,128)(2,1)S(1)} %collective-permute-done.far_ref, bf16[8,6,128,128]{3,2,1,0:T(8,128)(2,1)S(1)} %copy-done, ...), custom_call_target="tpu_custom_call" | custom-call | flops 25165824 | bytes 2000000 | tf_op jit(solution)/shard_map/pallas_call | solution.py:172
  18.5 16.1 %all_to_all.15.packed_ref = bf16[8,96,128]{2,1,0:T(8,128)(2,1)S(1)} all-to-all(bf16[8,96,128]{2,1,0:T(8,128)(2,1)S(1)} %shard_map.112), channel_id=1, replica_groups=mesh['x'=4,'z'=4,'near'=2,'c'=2,'feat'=8] {'feat'}, dimensions={0} | all-to-all | bytes 393216 | tf_op jit(solution)/shard_map/all_to_all | solution.py:180
  34.5 0.0 copy-done.1
  34.5 0.0 copy-done.6
  34.5 0.2 shard_map.113
  34.8 3.6 %all-gather.1 = bf16[1024,128]{1,0:T(8,128)(2,1)S(1)} all-gather(bf16[512,128]{1,0:T(8,128)(2,1)S(1)} %get-tuple-element.10), channel_id=3, replica_groups=mesh['x'=4,'z'=4,'near'=2,'c'=2,'feat'=8] {'c'}, dimensions={0}, use_global_device_ids=true | all-gather | bytes 393216 | tf_op jit(solution)/shard_map/all_gather | solution.py:193
  38.4 0.2 shard_map.114
  38.6 10.1 %all_to_all.16.rows_ref = bf16[16,9,2,128]{3,2,1,0:T(2,128)(2,1)S(1)} all-to-all(bf16[16,9,2,128]{3,2,1,0:T(2,128)(2,1)S(1)} %bitcast.12), channel_id=1, replica_groups=mesh['x'=4,'z'=4,'near'=2,'c'=2,'feat'=8] {'near','feat'}, dimensions={0} | all-to-all | bytes 147456 | tf_op jit(solution)/shard_map/all_to_all | solution.py:201
  48.6 0.1 shard_map.115
  48.7 12.5 %all_to_all.17.rows_ref = bf16[32,9,2,128]{3,2,1,0:T(2,128)(2,1)S(1)} all-to-all(bf16[32,9,2,128]{3,2,1,0:T(2,128)(2,1)S(1)} %shard_map.115), channel_id=1, replica_groups=mesh['x'=4,'z'=4,'near'=2,'c'=2,'feat'=8] {'x','z','near'}, dimensions={0} | all-to-all | bytes 294912 | tf_op jit(solution)/shard_map/all_to_all | solution.py:203
  61.3 0.1 shard_map.116
  61.3 4.7 %all-gather.2 = f32[80,128]{1,0:T(8,128)S(1)} all-gather(f32[40,128]{1,0:T(8,128)S(1)} %shard_map.116), channel_id=4, replica_groups=mesh['x'=4,'z'=4,'near'=2,'c'=2,'feat'=8] {'c'}, dimensions={0}, use_global_device_ids=true | all-gather | bytes 61440 | tf_op jit(solution)/shard_map/all_gather | solution.py:205
  66.1 0.6 shard_map.117
  (1 shorter events, 0.0 us)
Async XLA Ops:
  0.6 16.7 %collective-permute-start = (bf16[16,1024]{1,0:T(8,128)(2,1)}, bf16[16,1024]{1,0:T(8,128)(2,1)S(1)}, u32[]{:S(2)}, u32[]{:S(2)}) collective-permute-start(bf16[16,1024]{1,0:T(8,128)(2,1)} %bitcast.17), channel_id=1, source_target_pairs={{0,504},{8,16},{16,8},{24,32},{32,24},{40,48},{48,40},{56,64},{64,... | collective-permute-start | bytes 98312 | tf_op jit(solution)/shard_map/ppermute | solution.py:161
  6.2 0.8 %copy-start.7 = (bf16[1024,16]{0,1:T(8,128)(2,1)S(1)}, bf16[1024,16]{0,1:T(8,128)(2,1)}, u32[]{:S(2)}) copy-start(bf16[1024,16]{0,1:T(8,128)(2,1)} %param.8) | copy-start | bytes 98308
  6.2 11.1 %copy-start = (bf16[8,6,128,128]{3,2,1,0:T(8,128)(2,1)S(1)}, bf16[8,6,128,128]{3,2,1,0:T(8,128)(2,1)}, u32[]{:S(2)}) copy-start(bf16[8,6,128,128]{3,2,1,0:T(8,128)(2,1)} %adj_ref.1) | copy-start | bytes 4718596
  6.2 11.1 %copy-start.2 = (bf16[16,256]{1,0:T(8,128)(2,1)S(1)}, bf16[16,256]{1,0:T(8,128)(2,1)}, u32[]{:S(2)}) copy-start(bf16[16,256]{1,0:T(8,128)(2,1)} %ws_ref.1) | copy-start | bytes 24580
  6.2 11.1 %copy-start.3 = (bf16[16,256]{1,0:T(8,128)(2,1)S(1)}, bf16[16,256]{1,0:T(8,128)(2,1)}, u32[]{:S(2)}) copy-start(bf16[16,256]{1,0:T(8,128)(2,1)} %wn_ref.1) | copy-start | bytes 24580
  6.2 11.1 %copy-start.4 = (s32[8,6]{1,0:T(8,128)S(1)}, s32[8,6]{1,0:T(8,128)}, u32[]{:S(2)}) copy-start(s32[8,6]{1,0:T(8,128)} %cols_ref.1) | copy-start | bytes 580
  6.2 11.1 %copy-start.5 = (s32[1024]{0:T(1024)S(1)}, s32[1024]{0:T(1024)}, u32[]{:S(2)}) copy-start(s32[1024]{0:T(1024)} %param.11) | copy-start | bytes 12292
  7.0 27.6 %copy-start.1 = (bf16[128,256]{1,0:T(8,128)(2,1)S(1)}, bf16[128,256]{1,0:T(8,128)(2,1)}, u32[]{:S(2)}) copy-start(bf16[128,256]{1,0:T(8,128)(2,1)} %cot_ref.1) | copy-start | bytes 196612
  7.0 27.6 %copy-start.6 = (f32[256]{0:T(256)S(1)}, f32[256]{0:T(256)}, u32[]{:S(2)}) copy-start(f32[256]{0:T(256)} %param.14) | copy-start | bytes 3076

commit v6 on v5

--- a/solution.py
+++ b/solution.py
@@ -46,6 +46,7 @@
     first = place_ref[0, 0]
     turn = place_ref[1, 0]
     own = place_ref[2, 0]
+    weights_here = [jnp.where(own == 0, ref[:, :half], ref[:, half:]) for ref in (ws_ref, wn_ref)]
 
     def spot(col):
         col = col - first + blocks
@@ -60,47 +61,45 @@
         degree = deg_ref[:, r * size : (r + 1) * size].astype(F32)
         out_ref[r, :width] = feats[own + r]
         out_ref[r, width : 2 * width] = (total / degree).astype(BF16)
-        for h in range(2):
-            at = 2 * width * (1 + h)
-            out_ref[r, at : at + width] = ws_ref[:, h * half : (h + 1) * half]
-            out_ref[r, at + width : at + 2 * width] = wn_ref[:, h * half : (h + 1) * half]
-
-
-def forward_kernel(width, packed_ref, cot_ref, bias_ref, hidden_ref, share_ref):
-    feat_count = packed_ref.shape[0]
+        for i, part in enumerate(weights_here):
+            out_ref[r, (2 + i) * width : (3 + i) * width] = part
+
+
+def share_kernel(packed_ref, cot_ref, share_ref):
+    feat_count, depth, rows = packed_ref.shape
+    depth = feat_count * depth // 2
+    share_ref[:depth] = packed_ref[:, : depth // feat_count].reshape(depth, rows)
+    share_ref[depth : 2 * depth] = packed_ref[:, depth // feat_count :].reshape(depth, rows)
+    for h in range(2):
+        share_ref[2 * depth + h * rows : 2 * depth + (h + 1) * rows] = cot_ref[:, h * rows : (h + 1) * rows]
+
+
+def layer_kernel(packed_ref, pair_ref, place_ref, bias_ref, hidden_ref, grads_ref):
+    _, feat_count, pairs, _, half = grads_ref.shape
+    pairs -= 1
     rows = packed_ref.shape[2]
-    depth = feat_count * 2 * width
-    half = rows
-    inputs = packed_ref[:, : 2 * width].reshape(depth, rows)
-    left = packed_ref[:, 2 * width : 4 * width].reshape(depth, half)
-    right = packed_ref[:, 4 * width : 6 * width].reshape(depth, half)
-    share_ref[:depth] = inputs
-    for h, weights in enumerate((left, right)):
+    depth = feat_count * 4 * pairs
+    cots = 2 * depth
+    core = place_ref[2:3]
+    inputs = packed_ref[:, : 4 * pairs].reshape(depth, rows)
+    weights = packed_ref[:, 4 * pairs :].reshape(depth, half)
+    for h in range(2):
         lanes = slice(h * half, (h + 1) * half)
-        preact = lax.dot_general(inputs, weights, TN, preferred_element_type=F32) + bias_ref[:, lanes]
+        preact = lax.dot_general(inputs, pair_ref[h, depth:cots], TN, preferred_element_type=F32) + bias_ref[:, lanes]
         hidden_ref[:, lanes] = jnp.maximum(preact, 0.0).astype(BF16)
-        cot = cot_ref[:, lanes].astype(F32)
-        share_ref[depth + h * rows : depth + (h + 1) * rows] = jnp.where(preact > 0, cot, 0.0).astype(BF16)
-
-
-def backward_kernel(width, pair_ref, place_ref, grads_ref):
-    feat_count = grads_ref.shape[1]
-    pairs = width // 2
-    depth = feat_count * 2 * width
-    rows = (pair_ref.shape[1] - depth) // 2
-    core = jnp.broadcast_to(place_ref[2:3], (rows, pair_ref.shape[2]))
+    bias = jnp.where(core == 0, bias_ref[:, :half], bias_ref[:, half:])
+    core = jnp.broadcast_to(core, (rows, half))
+    grad_pre = []
+    for c in range(2):
+        preact = lax.dot_general(pair_ref[c, :depth], weights, TN, preferred_element_type=F32) + bias
+        cot = jnp.where(
+            core == 0,
+            pair_ref[c, cots : cots + rows].astype(F32),
+            pair_ref[c, cots + rows :].astype(F32),
+        )
+        grad_pre.append(jnp.where(preact > 0, cot, 0.0).astype(BF16))
+    grad_pre = jnp.concatenate(grad_pre, axis=0)
     inputs = jnp.concatenate([pair_ref[c, :depth] for c in range(2)], axis=1)
-    grad_pre = jnp.concatenate(
-        [
-            jnp.where(
-                core == 0,
-                pair_ref[c, depth : depth + rows].astype(F32),
-                pair_ref[c, depth + rows :].astype(F32),
-            ).astype(BF16)
-            for c in range(2)
-        ],
-        axis=0,
-    )
     grads = jnp.dot(inputs, grad_pre, preferred_element_type=F32)
     ones = jnp.ones((8, 2 * rows), BF16)
     bias = jnp.dot(ones, grad_pre, preferred_element_type=F32)[:1]
@@ -108,7 +107,7 @@
     for f in range(feat_count):
         for near in range(2):
             for i in range(pairs):
-                first = (f * 2 + near) * width + 2 * i
+                first = (f * 2 + near) * 2 * pairs + 2 * i
                 grads_ref[near, f, i] = grads[first : first + 2].astype(BF16)
             grads_ref[near, f, pairs] = bias
 
@@ -171,7 +170,7 @@
     )(jnp.broadcast_to(where[:, None], (3, size)))
     packed = call(
         functools.partial(aggregate_kernel, blocks * vertex_count),
-        jax.ShapeDtypeStruct((feat_count, 6 * width, rows_own), BF16),
+        jax.ShapeDtypeStruct((feat_count, 4 * width, rows_own), BF16),
         [SMEM] * 2 + [VMEM] * 6,
         [pltpu.VMEM((3 * blocks, width, size), BF16)],
         flops=2 * blocks * tiles * size * size * width,
@@ -181,22 +180,21 @@
     near_count = lax.axis_size("near")
     depth = feat_count * 2 * width
     pieces = (width // 2 + 1, 2, rows_own)
-    hidden, share = call(
-        functools.partial(forward_kernel, width),
+    share = call(
+        share_kernel,
+        jax.ShapeDtypeStruct((2 * depth + 2 * rows_own, rows_own), BF16),
+        [VMEM] * 2,
+    )(packed, cotangent)
+    pair = lax.all_gather(share, "c")
+    hidden, grads = call(
+        layer_kernel,
         (
             jax.ShapeDtypeStruct((rows_own, hidden_units), BF16),
-            jax.ShapeDtypeStruct((depth + 2 * rows_own, rows_own), BF16),
+            jax.ShapeDtypeStruct((near_count, feat_count, *pieces), BF16),
         ),
-        [VMEM] * 3,
-        flops=2 * rows_own * depth * hidden_units,
-    )(packed, cotangent, hidden_bias.reshape(1, -1))
-    pair = lax.all_gather(share, "c")
-    grads = call(
-        functools.partial(backward_kernel, width),
-        jax.ShapeDtypeStruct((near_count, feat_count, *pieces), BF16),
-        [VMEM] * 2,
-        flops=2 * rows_own * depth * hidden_units,
-    )(pair, place)
+        [VMEM] * 4,
+        flops=6 * rows_own * depth * hidden_units,
+    )(packed, pair, place, hidden_bias.reshape(1, -1))
 
     grads = lax.all_to_all(grads.reshape(near_count * feat_count, *pieces), ("near", "feat"), 0, 0, tiled=True)
     grads = call(sum_kernel, jax.ShapeDtypeStruct((chip_count, *pieces), BF16), [VMEM])(grads)

time: 67 us -> 65.7 us (0.981)
  blocking collectives: 57.3 us -> 56 us
    all_to_all x1, blocking collectives: 16.1 us -> 14.5 us  [shards(): packed = lax.all_to_all(packed, 'feat', 0, 0, tiled=True)]
where the time goes in v6:
time: 65.7 us; the launch traced here: 65.4 us
  blocking collectives  56 us (85%)
  starting transfers between devices  5.39 us (8%)
  Pallas kernels  2.47 us (4%)
  local copies, waits for them, and re-layouts  0.82 us (1%)
  between operations  0.72 us (1%)
    all_to_all x1, blocking collectives, shards(): packed = lax.all_to_all(packed, 'feat', 0, 0, tiled=True)  14.5 us
    all_to_all x1, blocking collectives, shards(): grads = lax.all_to_all(grads, CHIPS, 0, 0, tiled=True)  12.7 us
    all_gather x1, blocking collectives, shards(): pair = lax.all_gather(feats, 'c')  10.3 us
    all_to_all x1, blocking collectives, shards(): lax.all_to_all(grads.reshape(near_count * feat_count, *pieces), ('near',...  10.1 us
    ppermute x1, starting transfers between devices, shards(): far = lax.ppermute(feats, VERTEX, away)  5.39 us
    all_gather x1, blocking collectives, shards(): pair = lax.all_gather(grads, 'c')  4.52 us
    all_gather x1, blocking collectives, shards(): pair = lax.all_gather(share, 'c')  3.82 us
  transfers between devices with their start and end apart: 1, of which 0 were waited for; matrix products, arithmetic and copies ran while one was open for 0% of the time, Pallas kernels for 0%

profile of v6, /device:TPU:1, one launch (start us, length us, event | category | flops | bytes accessed | tf_op | source)
XLA Modules:
  0.0 65.4 jit_solution(1273468363674506237)
XLA Ops:
  0.6 5.4 %collective-permute-start = (bf16[16,1024]{1,0:T(8,128)(2,1)}, bf16[16,1024]{1,0:T(8,128)(2,1)S(1)}, u32[]{:S(2)}, u32[]{:S(2)}) collective-permute-start(bf16[16,1024]{1,0:T(8,128)(2,1)} %bitcast.17), channel_id=1, source_target_pairs={{0,504},{8,16},{16,8},{24,32},{32,24},{40,48},{48,40},{56,64},{64,... | collective-permute-start | bytes 98312 | tf_op jit(solution)/shard_map/ppermute | solution.py:160
  6.0 0.1 pad_add_fusion
  6.1 0.1 broadcast_in_dim.2.where_ref
  6.2 0.0 copy-start.7
  6.2 0.0 copy-start
  6.2 0.0 copy-start.2
  6.2 0.0 copy-start.3
  6.2 0.0 copy-start.4
  6.2 0.0 copy-start.5
  6.2 0.7 %copy-done.7 = bf16[1024,16]{0,1:T(8,128)(2,1)S(1)} copy-done((bf16[1024,16]{0,1:T(8,128)(2,1)S(1)}, bf16[1024,16]{0,1:T(8,128)(2,1)}, u32[]{:S(2)}) %copy-start.7) | copy-done | bytes 32792
  7.0 0.0 copy-start.1
  7.0 0.0 copy-start.6
  7.0 10.3 %all-gather = bf16[32,1024]{1,0:T(8,128)(2,1)S(1)} all-gather(bf16[16,1024]{1,0:T(8,128)(2,1)S(1)} %bitcast.18), channel_id=2, replica_groups=mesh['x'=4,'z'=4,'near'=2,'c'=2,'feat'=8] {'c'}, dimensions={0}, use_global_device_ids=true | all-gather | bytes 98304 | tf_op jit(solution)/shard_map/all_gather | solution.py:161
  17.3 0.0 collective-permute-done.far_ref
  17.3 0.0 copy-done
  17.3 0.0 copy-done.2
  17.3 0.0 copy-done.3
  17.3 0.0 copy-done.4
  17.3 0.0 copy-done.5
  17.3 1.1 %shard_map.112 = bf16[8,64,128]{2,1,0:T(8,128)(2,1)S(1)} custom-call(s32[8,6]{1,0:T(8,128)S(1)} %copy-done.4, s32[3,128]{1,0:T(4,128)S(1)} %shard_map.111.place_ref, bf16[2,16,1024]{2,1,0:T(8,128)(2,1)S(1)} %bitcast.12, bf16[16,1024]{1,0:T(8,128)(2,1)S(1)} %collective-permute-done.far_ref, bf16[8,6,128,128]{3,2,1,0:T(8,128)(2,1)S(1)} %copy-done, ...), custom_call_target="tpu_custom_call" | custom-call | flops 25165824 | bytes 2000000 | tf_op jit(solution)/shard_map/pallas_call | solution.py:171
  18.5 14.5 %all_to_all.15.packed_ref = bf16[8,64,128]{2,1,0:T(8,128)(2,1)S(1)} all-to-all(bf16[8,64,128]{2,1,0:T(8,128)(2,1)S(1)} %shard_map.112), channel_id=1, replica_groups=mesh['x'=4,'z'=4,'near'=2,'c'=2,'feat'=8] {'feat'}, dimensions={0} | all-to-all | bytes 262144 | tf_op jit(solution)/shard_map/all_to_all | solution.py:179
  33.0 0.0 copy-done.1
  33.0 3.8 %all-gather.1 = bf16[1536,128]{1,0:T(8,128)(2,1)S(1)} all-gather(bf16[768,128]{1,0:T(8,128)(2,1)S(1)} %shard_map.113), channel_id=3, replica_groups=mesh['x'=4,'z'=4,'near'=2,'c'=2,'feat'=8] {'c'}, dimensions={0}, use_global_device_ids=true | all-gather | bytes 589824 | tf_op jit(solution)/shard_map/all_gather | solution.py:188
  36.9 0.0 copy-done.6
  36.9 0.5 shard_map.114
  37.3 10.1 %all_to_all.16.rows_ref = bf16[16,9,2,128]{3,2,1,0:T(2,128)(2,1)S(1)} all-to-all(bf16[16,9,2,128]{3,2,1,0:T(2,128)(2,1)S(1)} %bitcast.14), channel_id=1, replica_groups=mesh['x'=4,'z'=4,'near'=2,'c'=2,'feat'=8] {'near','feat'}, dimensions={0} | all-to-all | bytes 147456 | tf_op jit(solution)/shard_map/all_to_all | solution.py:199
  47.4 0.1 shard_map.115
  47.5 12.7 %all_to_all.17.rows_ref = bf16[32,9,2,128]{3,2,1,0:T(2,128)(2,1)S(1)} all-to-all(bf16[32,9,2,128]{3,2,1,0:T(2,128)(2,1)S(1)} %shard_map.115), channel_id=1, replica_groups=mesh['x'=4,'z'=4,'near'=2,'c'=2,'feat'=8] {'x','z','near'}, dimensions={0} | all-to-all | bytes 294912 | tf_op jit(solution)/shard_map/all_to_all | solution.py:201
  60.2 0.1 shard_map.116
  60.3 4.5 %all-gather.2 = f32[80,128]{1,0:T(8,128)S(1)} all-gather(f32[40,128]{1,0:T(8,128)S(1)} %shard_map.116), channel_id=4, replica_groups=mesh['x'=4,'z'=4,'near'=2,'c'=2,'feat'=8] {'c'}, dimensions={0}, use_global_device_ids=true | all-gather | bytes 61440 | tf_op jit(solution)/shard_map/all_gather | solution.py:203
  64.8 0.6 shard_map.117
  (2 shorter events, 0.0 us)
Async XLA Ops:
  0.6 16.7 %collective-permute-start = (bf16[16,1024]{1,0:T(8,128)(2,1)}, bf16[16,1024]{1,0:T(8,128)(2,1)S(1)}, u32[]{:S(2)}, u32[]{:S(2)}) collective-permute-start(bf16[16,1024]{1,0:T(8,128)(2,1)} %bitcast.17), channel_id=1, source_target_pairs={{0,504},{8,16},{16,8},{24,32},{32,24},{40,48},{48,40},{56,64},{64,... | collective-permute-start | bytes 98312 | tf_op jit(solution)/shard_map/ppermute | solution.py:160
  6.2 0.8 %copy-start.7 = (bf16[1024,16]{0,1:T(8,128)(2,1)S(1)}, bf16[1024,16]{0,1:T(8,128)(2,1)}, u32[]{:S(2)}) copy-start(bf16[1024,16]{0,1:T(8,128)(2,1)} %param.8) | copy-start | bytes 98308
  6.2 11.1 %copy-start = (bf16[8,6,128,128]{3,2,1,0:T(8,128)(2,1)S(1)}, bf16[8,6,128,128]{3,2,1,0:T(8,128)(2,1)}, u32[]{:S(2)}) copy-start(bf16[8,6,128,128]{3,2,1,0:T(8,128)(2,1)} %adj_ref.1) | copy-start | bytes 4718596
  6.2 11.1 %copy-start.2 = (bf16[16,256]{1,0:T(8,128)(2,1)S(1)}, bf16[16,256]{1,0:T(8,128)(2,1)}, u32[]{:S(2)}) copy-start(bf16[16,256]{1,0:T(8,128)(2,1)} %ws_ref.1) | copy-start | bytes 24580
  6.2 11.1 %copy-start.3 = (bf16[16,256]{1,0:T(8,128)(2,1)S(1)}, bf16[16,256]{1,0:T(8,128)(2,1)}, u32[]{:S(2)}) copy-start(bf16[16,256]{1,0:T(8,128)(2,1)} %wn_ref.1) | copy-start | bytes 24580
  6.2 11.1 %copy-start.4 = (s32[8,6]{1,0:T(8,128)S(1)}, s32[8,6]{1,0:T(8,128)}, u32[]{:S(2)}) copy-start(s32[8,6]{1,0:T(8,128)} %cols_ref.1) | copy-start | bytes 580
  6.2 11.1 %copy-start.5 = (s32[1024]{0:T(1024)S(1)}, s32[1024]{0:T(1024)}, u32[]{:S(2)}) copy-start(s32[1024]{0:T(1024)} %param.11) | copy-start | bytes 12292
  7.0 26.1 %copy-start.1 = (bf16[128,256]{1,0:T(8,128)(2,1)S(1)}, bf16[128,256]{1,0:T(8,128)(2,1)}, u32[]{:S(2)}) copy-start(bf16[128,256]{1,0:T(8,128)(2,1)} %cot_ref.1) | copy-start | bytes 196612
  7.0 29.9 %copy-start.6 = (f32[256]{0:T(256)S(1)}, f32[256]{0:T(256)}, u32[]{:S(2)}) copy-start(f32[256]{0:T(256)} %param.14) | copy-start | bytes 3076

commit v7 on v6

--- a/solution.py
+++ b/solution.py
@@ -83,23 +83,22 @@
     core = place_ref[2:3]
     inputs = packed_ref[:, : 4 * pairs].reshape(depth, rows)
     weights = packed_ref[:, 4 * pairs :].reshape(depth, half)
-    for h in range(2):
-        lanes = slice(h * half, (h + 1) * half)
-        preact = lax.dot_general(inputs, pair_ref[h, depth:cots], TN, preferred_element_type=F32) + bias_ref[:, lanes]
-        hidden_ref[:, lanes] = jnp.maximum(preact, 0.0).astype(BF16)
+    units = jnp.concatenate([pair_ref[h, depth:cots] for h in range(2)], axis=1)
+    preact = lax.dot_general(inputs, units, TN, preferred_element_type=F32) + bias_ref[...]
+    hidden_ref[...] = jnp.maximum(preact, 0.0).astype(BF16)
     bias = jnp.where(core == 0, bias_ref[:, :half], bias_ref[:, half:])
     core = jnp.broadcast_to(core, (rows, half))
+    inputs = jnp.concatenate([pair_ref[c, :depth] for c in range(2)], axis=1)
+    preact = lax.dot_general(inputs, weights, TN, preferred_element_type=F32) + bias
     grad_pre = []
     for c in range(2):
-        preact = lax.dot_general(pair_ref[c, :depth], weights, TN, preferred_element_type=F32) + bias
         cot = jnp.where(
             core == 0,
             pair_ref[c, cots : cots + rows].astype(F32),
             pair_ref[c, cots + rows :].astype(F32),
         )
-        grad_pre.append(jnp.where(preact > 0, cot, 0.0).astype(BF16))
+        grad_pre.append(jnp.where(preact[c * rows : (c + 1) * rows] > 0, cot, 0.0).astype(BF16))
     grad_pre = jnp.concatenate(grad_pre, axis=0)
-    inputs = jnp.concatenate([pair_ref[c, :depth] for c in range(2)], axis=1)
     grads = jnp.dot(inputs, grad_pre, preferred_element_type=F32)
     ones = jnp.ones((8, 2 * rows), BF16)
     bias = jnp.dot(ones, grad_pre, preferred_element_type=F32)[:1]

time: 65.7 us -> 65.7 us (level)
  no operation moved by 1% of the time
where the time goes in v7:
time: 65.7 us; the launch traced here: 65.4 us
  blocking collectives  56 us (85%)
  starting transfers between devices  5.39 us (8%)
  Pallas kernels  2.41 us (4%)
  local copies, waits for them, and re-layouts  0.82 us (1%)
  between operations  0.72 us (1%)
    all_to_all x1, blocking collectives, shards(): packed = lax.all_to_all(packed, 'feat', 0, 0, tiled=True)  14.5 us
    all_to_all x1, blocking collectives, shards(): grads = lax.all_to_all(grads, CHIPS, 0, 0, tiled=True)  12.7 us
    all_gather x1, blocking collectives, shards(): pair = lax.all_gather(feats, 'c')  10.3 us
    all_to_all x1, blocking collectives, shards(): lax.all_to_all(grads.reshape(near_count * feat_count, *pieces), ('near',...  10.1 us
    ppermute x1, starting transfers between devices, shards(): far = lax.ppermute(feats, VERTEX, away)  5.39 us
    all_gather x1, blocking collectives, shards(): pair = lax.all_gather(grads, 'c')  4.52 us
    all_gather x1, blocking collectives, shards(): pair = lax.all_gather(share, 'c')  3.82 us
  transfers between devices with their start and end apart: 1, of which 0 were waited for; matrix products, arithmetic and copies ran while one was open for 0% of the time, Pallas kernels for 0%

profile of v7, /device:TPU:1, one launch (start us, length us, event | category | flops | bytes accessed | tf_op | source)
XLA Modules:
  0.0 65.4 jit_solution(4235131598925029281)
XLA Ops:
  0.6 5.4 %collective-permute-start = (bf16[16,1024]{1,0:T(8,128)(2,1)}, bf16[16,1024]{1,0:T(8,128)(2,1)S(1)}, u32[]{:S(2)}, u32[]{:S(2)}) collective-permute-start(bf16[16,1024]{1,0:T(8,128)(2,1)} %bitcast.17), channel_id=1, source_target_pairs={{0,504},{8,16},{16,8},{24,32},{32,24},{40,48},{48,40},{56,64},{64,... | collective-permute-start | bytes 98312 | tf_op jit(solution)/shard_map/ppermute | solution.py:159
  6.0 0.1 pad_add_fusion
  6.1 0.1 broadcast_in_dim.2.where_ref
  6.2 0.0 copy-start.7
  6.2 0.0 copy-start
  6.2 0.0 copy-start.2
  6.2 0.0 copy-start.3
  6.2 0.0 copy-start.4
  6.2 0.0 copy-start.5
  6.2 0.7 %copy-done.7 = bf16[1024,16]{0,1:T(8,128)(2,1)S(1)} copy-done((bf16[1024,16]{0,1:T(8,128)(2,1)S(1)}, bf16[1024,16]{0,1:T(8,128)(2,1)}, u32[]{:S(2)}) %copy-start.7) | copy-done | bytes 32792
  7.0 0.0 copy-start.1
  7.0 0.0 copy-start.6
  7.0 10.3 %all-gather = bf16[32,1024]{1,0:T(8,128)(2,1)S(1)} all-gather(bf16[16,1024]{1,0:T(8,128)(2,1)S(1)} %bitcast.18), channel_id=2, replica_groups=mesh['x'=4,'z'=4,'near'=2,'c'=2,'feat'=8] {'c'}, dimensions={0}, use_global_device_ids=true | all-gather | bytes 98304 | tf_op jit(solution)/shard_map/all_gather | solution.py:160
  17.3 0.0 collective-permute-done.far_ref
  17.3 0.0 copy-done
  17.3 0.0 copy-done.2
  17.3 0.0 copy-done.3
  17.3 0.0 copy-done.4
  17.3 0.0 copy-done.5
  17.3 1.1 %shard_map.112 = bf16[8,64,128]{2,1,0:T(8,128)(2,1)S(1)} custom-call(s32[8,6]{1,0:T(8,128)S(1)} %copy-done.4, s32[3,128]{1,0:T(4,128)S(1)} %shard_map.111.place_ref, bf16[2,16,1024]{2,1,0:T(8,128)(2,1)S(1)} %bitcast.12, bf16[16,1024]{1,0:T(8,128)(2,1)S(1)} %collective-permute-done.far_ref, bf16[8,6,128,128]{3,2,1,0:T(8,128)(2,1)S(1)} %copy-done, ...), custom_call_target="tpu_custom_call" | custom-call | flops 25165824 | bytes 2000000 | tf_op jit(solution)/shard_map/pallas_call | solution.py:170
  18.5 14.5 %all_to_all.15.packed_ref = bf16[8,64,128]{2,1,0:T(8,128)(2,1)S(1)} all-to-all(bf16[8,64,128]{2,1,0:T(8,128)(2,1)S(1)} %shard_map.112), channel_id=1, replica_groups=mesh['x'=4,'z'=4,'near'=2,'c'=2,'feat'=8] {'feat'}, dimensions={0} | all-to-all | bytes 262144 | tf_op jit(solution)/shard_map/all_to_all | solution.py:178
  33.0 0.0 copy-done.1
  33.0 3.8 %all-gather.1 = bf16[1536,128]{1,0:T(8,128)(2,1)S(1)} all-gather(bf16[768,128]{1,0:T(8,128)(2,1)S(1)} %shard_map.113), channel_id=3, replica_groups=mesh['x'=4,'z'=4,'near'=2,'c'=2,'feat'=8] {'c'}, dimensions={0}, use_global_device_ids=true | all-gather | bytes 589824 | tf_op jit(solution)/shard_map/all_gather | solution.py:187
  36.9 0.0 copy-done.6
  36.9 0.4 shard_map.114
  37.3 10.1 %all_to_all.16.rows_ref = bf16[16,9,2,128]{3,2,1,0:T(2,128)(2,1)S(1)} all-to-all(bf16[16,9,2,128]{3,2,1,0:T(2,128)(2,1)S(1)} %bitcast.14), channel_id=1, replica_groups=mesh['x'=4,'z'=4,'near'=2,'c'=2,'feat'=8] {'near','feat'}, dimensions={0} | all-to-all | bytes 147456 | tf_op jit(solution)/shard_map/all_to_all | solution.py:198
  47.3 0.1 shard_map.115
  47.4 12.7 %all_to_all.17.rows_ref = bf16[32,9,2,128]{3,2,1,0:T(2,128)(2,1)S(1)} all-to-all(bf16[32,9,2,128]{3,2,1,0:T(2,128)(2,1)S(1)} %shard_map.115), channel_id=1, replica_groups=mesh['x'=4,'z'=4,'near'=2,'c'=2,'feat'=8] {'x','z','near'}, dimensions={0} | all-to-all | bytes 294912 | tf_op jit(solution)/shard_map/all_to_all | solution.py:200
  60.1 0.1 shard_map.116
  60.2 4.5 %all-gather.2 = f32[80,128]{1,0:T(8,128)S(1)} all-gather(f32[40,128]{1,0:T(8,128)S(1)} %shard_map.116), channel_id=4, replica_groups=mesh['x'=4,'z'=4,'near'=2,'c'=2,'feat'=8] {'c'}, dimensions={0}, use_global_device_ids=true | all-gather | bytes 61440 | tf_op jit(solution)/shard_map/all_gather | solution.py:202
  64.7 0.6 shard_map.117
  (2 shorter events, 0.0 us)
Async XLA Ops:
  0.6 16.7 %collective-permute-start = (bf16[16,1024]{1,0:T(8,128)(2,1)}, bf16[16,1024]{1,0:T(8,128)(2,1)S(1)}, u32[]{:S(2)}, u32[]{:S(2)}) collective-permute-start(bf16[16,1024]{1,0:T(8,128)(2,1)} %bitcast.17), channel_id=1, source_target_pairs={{0,504},{8,16},{16,8},{24,32},{32,24},{40,48},{48,40},{56,64},{64,... | collective-permute-start | bytes 98312 | tf_op jit(solution)/shard_map/ppermute | solution.py:159
  6.2 0.8 %copy-start.7 = (bf16[1024,16]{0,1:T(8,128)(2,1)S(1)}, bf16[1024,16]{0,1:T(8,128)(2,1)}, u32[]{:S(2)}) copy-start(bf16[1024,16]{0,1:T(8,128)(2,1)} %param.8) | copy-start | bytes 98308
  6.2 11.1 %copy-start = (bf16[8,6,128,128]{3,2,1,0:T(8,128)(2,1)S(1)}, bf16[8,6,128,128]{3,2,1,0:T(8,128)(2,1)}, u32[]{:S(2)}) copy-start(bf16[8,6,128,128]{3,2,1,0:T(8,128)(2,1)} %adj_ref.1) | copy-start | bytes 4718596
  6.2 11.1 %copy-start.2 = (bf16[16,256]{1,0:T(8,128)(2,1)S(1)}, bf16[16,256]{1,0:T(8,128)(2,1)}, u32[]{:S(2)}) copy-start(bf16[16,256]{1,0:T(8,128)(2,1)} %ws_ref.1) | copy-start | bytes 24580
  6.2 11.1 %copy-start.3 = (bf16[16,256]{1,0:T(8,128)(2,1)S(1)}, bf16[16,256]{1,0:T(8,128)(2,1)}, u32[]{:S(2)}) copy-start(bf16[16,256]{1,0:T(8,128)(2,1)} %wn_ref.1) | copy-start | bytes 24580
  6.2 11.1 %copy-start.4 = (s32[8,6]{1,0:T(8,128)S(1)}, s32[8,6]{1,0:T(8,128)}, u32[]{:S(2)}) copy-start(s32[8,6]{1,0:T(8,128)} %cols_ref.1) | copy-start | bytes 580
  6.2 11.1 %copy-start.5 = (s32[1024]{0:T(1024)S(1)}, s32[1024]{0:T(1024)}, u32[]{:S(2)}) copy-start(s32[1024]{0:T(1024)} %param.11) | copy-start | bytes 12292
  7.0 26.1 %copy-start.1 = (bf16[128,256]{1,0:T(8,128)(2,1)S(1)}, bf16[128,256]{1,0:T(8,128)(2,1)}, u32[]{:S(2)}) copy-start(bf16[128,256]{1,0:T(8,128)(2,1)} %cot_ref.1) | copy-start | bytes 196612
  7.0 29.9 %copy-start.6 = (f32[256]{0:T(256)S(1)}, f32[256]{0:T(256)}, u32[]{:S(2)}) copy-start(f32[256]{0:T(256)} %param.14) | copy-start | bytes 3076

commit v8 on v7

--- a/solution.py
+++ b/solution.py
@@ -103,11 +103,10 @@
     ones = jnp.ones((8, 2 * rows), BF16)
     bias = jnp.dot(ones, grad_pre, preferred_element_type=F32)[:1]
     bias = jnp.concatenate([bias, jnp.zeros_like(bias)], axis=0).astype(BF16)
-    for f in range(feat_count):
-        for near in range(2):
-            for i in range(pairs):
-                first = (f * 2 + near) * 2 * pairs + 2 * i
-                grads_ref[near, f, i] = grads[first : first + 2].astype(BF16)
+    grads = grads.reshape(feat_count, 2, pairs, 2, half).astype(BF16)
+    for near in range(2):
+        grads_ref[near, :, :pairs] = grads[:, near]
+        for f in range(feat_count):
             grads_ref[near, f, pairs] = bias
 
 

time: 65.7 us -> 65.7 us (level)
  no operation moved by 1% of the time
where the time goes in v8:
time: 65.7 us; the launch traced here: 65.4 us
  blocking collectives  56 us (85%)
  starting transfers between devices  5.39 us (8%)
  Pallas kernels  2.41 us (4%)
  local copies, waits for them, and re-layouts  0.82 us (1%)
  between operations  0.72 us (1%)
    all_to_all x1, blocking collectives, shards(): packed = lax.all_to_all(packed, 'feat', 0, 0, tiled=True)  14.5 us
    all_to_all x1, blocking collectives, shards(): grads = lax.all_to_all(grads, CHIPS, 0, 0, tiled=True)  12.7 us
    all_gather x1, blocking collectives, shards(): pair = lax.all_gather(feats, 'c')  10.3 us
    all_to_all x1, blocking collectives, shards(): lax.all_to_all(grads.reshape(near_count * feat_count, *pieces), ('near',...  10.1 us
    ppermute x1, starting transfers between devices, shards(): far = lax.ppermute(feats, VERTEX, away)  5.39 us
    all_gather x1, blocking collectives, shards(): pair = lax.all_gather(grads, 'c')  4.52 us
    all_gather x1, blocking collectives, shards(): pair = lax.all_gather(share, 'c')  3.82 us
  transfers between devices with their start and end apart: 1, of which 0 were waited for; matrix products, arithmetic and copies ran while one was open for 0% of the time, Pallas kernels for 0%

profile of v8, /device:TPU:1, one launch (start us, length us, event | category | flops | bytes accessed | tf_op | source)
XLA Modules:
  0.0 65.4 jit_solution(815113174836510354)
XLA Ops:
  0.6 5.4 %collective-permute-start = (bf16[16,1024]{1,0:T(8,128)(2,1)}, bf16[16,1024]{1,0:T(8,128)(2,1)S(1)}, u32[]{:S(2)}, u32[]{:S(2)}) collective-permute-start(bf16[16,1024]{1,0:T(8,128)(2,1)} %bitcast.17), channel_id=1, source_target_pairs={{0,504},{8,16},{16,8},{24,32},{32,24},{40,48},{48,40},{56,64},{64,... | collective-permute-start | bytes 98312 | tf_op jit(solution)/shard_map/ppermute | solution.py:158
  6.0 0.1 pad_add_fusion
  6.1 0.1 broadcast_in_dim.2.where_ref
  6.2 0.0 copy-start.7
  6.2 0.0 copy-start
  6.2 0.0 copy-start.2
  6.2 0.0 copy-start.3
  6.2 0.0 copy-start.4
  6.2 0.0 copy-start.5
  6.2 0.7 %copy-done.7 = bf16[1024,16]{0,1:T(8,128)(2,1)S(1)} copy-done((bf16[1024,16]{0,1:T(8,128)(2,1)S(1)}, bf16[1024,16]{0,1:T(8,128)(2,1)}, u32[]{:S(2)}) %copy-start.7) | copy-done | bytes 32792
  7.0 0.0 copy-start.1
  7.0 0.0 copy-start.6
  7.0 10.3 %all-gather = bf16[32,1024]{1,0:T(8,128)(2,1)S(1)} all-gather(bf16[16,1024]{1,0:T(8,128)(2,1)S(1)} %bitcast.18), channel_id=2, replica_groups=mesh['x'=4,'z'=4,'near'=2,'c'=2,'feat'=8] {'c'}, dimensions={0}, use_global_device_ids=true | all-gather | bytes 98304 | tf_op jit(solution)/shard_map/all_gather | solution.py:159
  17.3 0.0 collective-permute-done.far_ref
  17.3 0.0 copy-done
  17.3 0.0 copy-done.2
  17.3 0.0 copy-done.3
  17.3 0.0 copy-done.4
  17.3 0.0 copy-done.5
  17.3 1.1 %shard_map.112 = bf16[8,64,128]{2,1,0:T(8,128)(2,1)S(1)} custom-call(s32[8,6]{1,0:T(8,128)S(1)} %copy-done.4, s32[3,128]{1,0:T(4,128)S(1)} %shard_map.111.place_ref, bf16[2,16,1024]{2,1,0:T(8,128)(2,1)S(1)} %bitcast.12, bf16[16,1024]{1,0:T(8,128)(2,1)S(1)} %collective-permute-done.far_ref, bf16[8,6,128,128]{3,2,1,0:T(8,128)(2,1)S(1)} %copy-done, ...), custom_call_target="tpu_custom_call" | custom-call | flops 25165824 | bytes 2000000 | tf_op jit(solution)/shard_map/pallas_call | solution.py:169
  18.5 14.5 %all_to_all.15.packed_ref = bf16[8,64,128]{2,1,0:T(8,128)(2,1)S(1)} all-to-all(bf16[8,64,128]{2,1,0:T(8,128)(2,1)S(1)} %shard_map.112), channel_id=1, replica_groups=mesh['x'=4,'z'=4,'near'=2,'c'=2,'feat'=8] {'feat'}, dimensions={0} | all-to-all | bytes 262144 | tf_op jit(solution)/shard_map/all_to_all | solution.py:177
  33.0 0.0 copy-done.1
  33.0 3.8 %all-gather.1 = bf16[1536,128]{1,0:T(8,128)(2,1)S(1)} all-gather(bf16[768,128]{1,0:T(8,128)(2,1)S(1)} %shard_map.113), channel_id=3, replica_groups=mesh['x'=4,'z'=4,'near'=2,'c'=2,'feat'=8] {'c'}, dimensions={0}, use_global_device_ids=true | all-gather | bytes 589824 | tf_op jit(solution)/shard_map/all_gather | solution.py:186
  36.9 0.0 copy-done.6
  36.9 0.4 shard_map.114
  37.3 10.1 %all_to_all.16.rows_ref = bf16[16,9,2,128]{3,2,1,0:T(2,128)(2,1)S(1)} all-to-all(bf16[16,9,2,128]{3,2,1,0:T(2,128)(2,1)S(1)} %bitcast.14), channel_id=1, replica_groups=mesh['x'=4,'z'=4,'near'=2,'c'=2,'feat'=8] {'near','feat'}, dimensions={0} | all-to-all | bytes 147456 | tf_op jit(solution)/shard_map/all_to_all | solution.py:197
  47.3 0.1 shard_map.115
  47.4 12.7 %all_to_all.17.rows_ref = bf16[32,9,2,128]{3,2,1,0:T(2,128)(2,1)S(1)} all-to-all(bf16[32,9,2,128]{3,2,1,0:T(2,128)(2,1)S(1)} %shard_map.115), channel_id=1, replica_groups=mesh['x'=4,'z'=4,'near'=2,'c'=2,'feat'=8] {'x','z','near'}, dimensions={0} | all-to-all | bytes 294912 | tf_op jit(solution)/shard_map/all_to_all | solution.py:199
  60.1 0.1 shard_map.116
  60.2 4.5 %all-gather.2 = f32[80,128]{1,0:T(8,128)S(1)} all-gather(f32[40,128]{1,0:T(8,128)S(1)} %shard_map.116), channel_id=4, replica_groups=mesh['x'=4,'z'=4,'near'=2,'c'=2,'feat'=8] {'c'}, dimensions={0}, use_global_device_ids=true | all-gather | bytes 61440 | tf_op jit(solution)/shard_map/all_gather | solution.py:201
  64.7 0.6 shard_map.117
  (2 shorter events, 0.0 us)
Async XLA Ops:
  0.6 16.7 %collective-permute-start = (bf16[16,1024]{1,0:T(8,128)(2,1)}, bf16[16,1024]{1,0:T(8,128)(2,1)S(1)}, u32[]{:S(2)}, u32[]{:S(2)}) collective-permute-start(bf16[16,1024]{1,0:T(8,128)(2,1)} %bitcast.17), channel_id=1, source_target_pairs={{0,504},{8,16},{16,8},{24,32},{32,24},{40,48},{48,40},{56,64},{64,... | collective-permute-start | bytes 98312 | tf_op jit(solution)/shard_map/ppermute | solution.py:158
  6.2 0.8 %copy-start.7 = (bf16[1024,16]{0,1:T(8,128)(2,1)S(1)}, bf16[1024,16]{0,1:T(8,128)(2,1)}, u32[]{:S(2)}) copy-start(bf16[1024,16]{0,1:T(8,128)(2,1)} %param.8) | copy-start | bytes 98308
  6.2 11.1 %copy-start = (bf16[8,6,128,128]{3,2,1,0:T(8,128)(2,1)S(1)}, bf16[8,6,128,128]{3,2,1,0:T(8,128)(2,1)}, u32[]{:S(2)}) copy-start(bf16[8,6,128,128]{3,2,1,0:T(8,128)(2,1)} %adj_ref.1) | copy-start | bytes 4718596
  6.2 11.1 %copy-start.2 = (bf16[16,256]{1,0:T(8,128)(2,1)S(1)}, bf16[16,256]{1,0:T(8,128)(2,1)}, u32[]{:S(2)}) copy-start(bf16[16,256]{1,0:T(8,128)(2,1)} %ws_ref.1) | copy-start | bytes 24580
  6.2 11.1 %copy-start.3 = (bf16[16,256]{1,0:T(8,128)(2,1)S(1)}, bf16[16,256]{1,0:T(8,128)(2,1)}, u32[]{:S(2)}) copy-start(bf16[16,256]{1,0:T(8,128)(2,1)} %wn_ref.1) | copy-start | bytes 24580
  6.2 11.1 %copy-start.4 = (s32[8,6]{1,0:T(8,128)S(1)}, s32[8,6]{1,0:T(8,128)}, u32[]{:S(2)}) copy-start(s32[8,6]{1,0:T(8,128)} %cols_ref.1) | copy-start | bytes 580
  6.2 11.1 %copy-start.5 = (s32[1024]{0:T(1024)S(1)}, s32[1024]{0:T(1024)}, u32[]{:S(2)}) copy-start(s32[1024]{0:T(1024)} %param.11) | copy-start | bytes 12292
  7.0 26.1 %copy-start.1 = (bf16[128,256]{1,0:T(8,128)(2,1)S(1)}, bf16[128,256]{1,0:T(8,128)(2,1)}, u32[]{:S(2)}) copy-start(bf16[128,256]{1,0:T(8,128)(2,1)} %cot_ref.1) | copy-start | bytes 196612
  7.0 29.9 %copy-start.6 = (f32[256]{0:T(256)S(1)}, f32[256]{0:T(256)}, u32[]{:S(2)}) copy-start(f32[256]{0:T(256)} %param.14) | copy-start | bytes 3076

commit v9 on v7

--- a/solution.py
+++ b/solution.py
@@ -165,7 +165,7 @@
         functools.partial(place_kernel, blocks),
         jax.ShapeDtypeStruct((3, size), jnp.int32),
         [VMEM],
-        flops=5 * 10**9,
+        flops=5 * 10**8,
     )(jnp.broadcast_to(where[:, None], (3, size)))
     packed = call(
         functools.partial(aggregate_kernel, blocks * vertex_count),

time: 65.7 us -> 65.8 us (level)
  local copies, waits for them, and re-layouts: 0.82 us -> 0.1 us
  blocking collectives: 56 us -> 56.7 us
    unnamed x16 -> x14, local copies, waits for them, and re-layouts: 0.75 us -> 0.03 us
where the time goes in v9:
time: 65.8 us; the launch traced here: 65.6 us
  blocking collectives  56.7 us (86%)
  starting transfers between devices  5.52 us (8%)
  Pallas kernels  2.41 us (4%)
  between operations  0.75 us (1%)
    all_to_all x1, blocking collectives, shards(): packed = lax.all_to_all(packed, 'feat', 0, 0, tiled=True)  14.6 us
    all_to_all x1, blocking collectives, shards(): grads = lax.all_to_all(grads, CHIPS, 0, 0, tiled=True)  13.3 us
    all_gather x1, blocking collectives, shards(): pair = lax.all_gather(feats, 'c')  10.4 us
    all_to_all x1, blocking collectives, shards(): lax.all_to_all(grads.reshape(near_count * feat_count, *pieces), ('near',...  10.1 us
    ppermute x1, starting transfers between devices, shards(): far = lax.ppermute(feats, VERTEX, away)  5.52 us
    all_gather x1, blocking collectives, shards(): pair = lax.all_gather(grads, 'c')  4.52 us
    all_gather x1, blocking collectives, shards(): pair = lax.all_gather(share, 'c')  3.81 us
  transfers between devices with their start and end apart: 1, of which 0 were waited for; matrix products, arithmetic and copies ran while one was open for 0% of the time, Pallas kernels for 0%

profile of v9, /device:TPU:1, one launch (start us, length us, event | category | flops | bytes accessed | tf_op | source)
XLA Modules:
  0.0 65.6 jit_solution(16073952973058194386)
XLA Ops:
  0.6 0.0 copy-start.3
  0.6 0.0 copy-start.2
  0.7 0.0 copy-start.5
  0.7 0.0 copy-start.4
  0.7 0.0 copy-start
  0.7 5.5 %collective-permute-start = (bf16[16,1024]{1,0:T(8,128)(2,1)}, bf16[16,1024]{1,0:T(8,128)(2,1)S(1)}, u32[]{:S(2)}, u32[]{:S(2)}) collective-permute-start(bf16[16,1024]{1,0:T(8,128)(2,1)} %bitcast.17), channel_id=1, source_target_pairs={{0,504},{8,16},{16,8},{24,32},{32,24},{40,48},{48,40},{56,64},{64,... | collective-permute-start | bytes 98312 | tf_op jit(solution)/shard_map/ppermute | solution.py:159
  6.2 10.4 %all-gather = bf16[32,1024]{1,0:T(8,128)(2,1)S(1)} all-gather(bf16[16,1024]{1,0:T(8,128)(2,1)} %bitcast.18), channel_id=2, replica_groups=mesh['x'=4,'z'=4,'near'=2,'c'=2,'feat'=8] {'c'}, dimensions={0}, use_global_device_ids=true | all-gather | bytes 98304 | tf_op jit(solution)/shard_map/all_gather | solution.py:160
  16.6 0.1 pad_add_fusion
  16.7 0.1 broadcast_in_dim.2.where_ref
  16.8 0.0 copy-start.1
  16.8 0.0 copy-start.6
  16.8 0.0 collective-permute-done.far_ref
  16.8 0.0 copy-done.3
  16.8 0.0 copy-done.2
  16.8 0.0 copy-done.5
  16.8 0.0 copy-done.4
  16.8 0.0 copy-done
  16.8 1.1 %shard_map.112 = bf16[8,64,128]{2,1,0:T(8,128)(2,1)S(1)} custom-call(s32[8,6]{1,0:T(8,128)S(1)} %copy-done.4, s32[3,128]{1,0:T(4,128)S(1)} %shard_map.111.place_ref, bf16[2,16,1024]{2,1,0:T(8,128)(2,1)S(1)} %bitcast.12, bf16[16,1024]{1,0:T(8,128)(2,1)S(1)} %collective-permute-done.far_ref, bf16[8,6,128,128]{3,2,1,0:T(8,128)(2,1)S(1)} %copy-done, ...), custom_call_target="tpu_custom_call" | custom-call | flops 25165824 | bytes 2000000 | tf_op jit(solution)/shard_map/pallas_call | solution.py:170
  18.0 14.6 %all_to_all.15.packed_ref = bf16[8,64,128]{2,1,0:T(8,128)(2,1)S(1)} all-to-all(bf16[8,64,128]{2,1,0:T(8,128)(2,1)S(1)} %shard_map.112), channel_id=1, replica_groups=mesh['x'=4,'z'=4,'near'=2,'c'=2,'feat'=8] {'feat'}, dimensions={0} | all-to-all | bytes 262144 | tf_op jit(solution)/shard_map/all_to_all | solution.py:178
  32.5 0.0 copy-done.1
  32.6 3.8 %all-gather.1 = bf16[1536,128]{1,0:T(8,128)(2,1)S(1)} all-gather(bf16[768,128]{1,0:T(8,128)(2,1)S(1)} %shard_map.113), channel_id=3, replica_groups=mesh['x'=4,'z'=4,'near'=2,'c'=2,'feat'=8] {'c'}, dimensions={0}, use_global_device_ids=true | all-gather | bytes 589824 | tf_op jit(solution)/shard_map/all_gather | solution.py:187
  36.4 0.0 copy-done.6
  36.4 0.4 shard_map.114
  36.8 10.1 %all_to_all.16.rows_ref = bf16[16,9,2,128]{3,2,1,0:T(2,128)(2,1)S(1)} all-to-all(bf16[16,9,2,128]{3,2,1,0:T(2,128)(2,1)S(1)} %bitcast.14), channel_id=1, replica_groups=mesh['x'=4,'z'=4,'near'=2,'c'=2,'feat'=8] {'near','feat'}, dimensions={0} | all-to-all | bytes 147456 | tf_op jit(solution)/shard_map/all_to_all | solution.py:198
  46.9 0.1 shard_map.115
  47.0 13.3 %all_to_all.17.rows_ref = bf16[32,9,2,128]{3,2,1,0:T(2,128)(2,1)S(1)} all-to-all(bf16[32,9,2,128]{3,2,1,0:T(2,128)(2,1)S(1)} %shard_map.115), channel_id=1, replica_groups=mesh['x'=4,'z'=4,'near'=2,'c'=2,'feat'=8] {'x','z','near'}, dimensions={0} | all-to-all | bytes 294912 | tf_op jit(solution)/shard_map/all_to_all | solution.py:200
  60.3 0.1 shard_map.116
  60.4 4.5 %all-gather.2 = f32[80,128]{1,0:T(8,128)S(1)} all-gather(f32[40,128]{1,0:T(8,128)S(1)} %shard_map.116), channel_id=4, replica_groups=mesh['x'=4,'z'=4,'near'=2,'c'=2,'feat'=8] {'c'}, dimensions={0}, use_global_device_ids=true | all-gather | bytes 61440 | tf_op jit(solution)/shard_map/all_gather | solution.py:202
  64.9 0.6 shard_map.117
  (2 shorter events, 0.0 us)
Async XLA Ops:
  0.6 16.2 %copy-start.3 = (bf16[16,256]{1,0:T(8,128)(2,1)S(1)}, bf16[16,256]{1,0:T(8,128)(2,1)}, u32[]{:S(2)}) copy-start(bf16[16,256]{1,0:T(8,128)(2,1)} %wn_ref.1) | copy-start | bytes 24580
  0.6 16.2 %copy-start.2 = (bf16[16,256]{1,0:T(8,128)(2,1)S(1)}, bf16[16,256]{1,0:T(8,128)(2,1)}, u32[]{:S(2)}) copy-start(bf16[16,256]{1,0:T(8,128)(2,1)} %ws_ref.1) | copy-start | bytes 24580
  0.7 16.2 %copy-start.5 = (s32[1024]{0:T(1024)S(1)}, s32[1024]{0:T(1024)}, u32[]{:S(2)}) copy-start(s32[1024]{0:T(1024)} %param.11) | copy-start | bytes 12292
  0.7 16.2 %copy-start.4 = (s32[8,6]{1,0:T(8,128)S(1)}, s32[8,6]{1,0:T(8,128)}, u32[]{:S(2)}) copy-start(s32[8,6]{1,0:T(8,128)} %cols_ref.1) | copy-start | bytes 580
  0.7 16.2 %copy-start = (bf16[8,6,128,128]{3,2,1,0:T(8,128)(2,1)S(1)}, bf16[8,6,128,128]{3,2,1,0:T(8,128)(2,1)}, u32[]{:S(2)}) copy-start(bf16[8,6,128,128]{3,2,1,0:T(8,128)(2,1)} %adj_ref.1) | copy-start | bytes 4718596
  0.7 16.1 %collective-permute-start = (bf16[16,1024]{1,0:T(8,128)(2,1)}, bf16[16,1024]{1,0:T(8,128)(2,1)S(1)}, u32[]{:S(2)}, u32[]{:S(2)}) collective-permute-start(bf16[16,1024]{1,0:T(8,128)(2,1)} %bitcast.17), channel_id=1, source_target_pairs={{0,504},{8,16},{16,8},{24,32},{32,24},{40,48},{48,40},{56,64},{64,... | collective-permute-start | bytes 98312 | tf_op jit(solution)/shard_map/ppermute | solution.py:159
  16.8 15.8 %copy-start.1 = (bf16[128,256]{1,0:T(8,128)(2,1)S(1)}, bf16[128,256]{1,0:T(8,128)(2,1)}, u32[]{:S(2)}) copy-start(bf16[128,256]{1,0:T(8,128)(2,1)} %cot_ref.1) | copy-start | bytes 196612
  16.8 19.6 %copy-start.6 = (f32[256]{0:T(256)S(1)}, f32[256]{0:T(256)}, u32[]{:S(2)}) copy-start(f32[256]{0:T(256)} %param.14) | copy-start | bytes 3076
